TPU v7x, 768 devices: a whole 4x8x12 slice. The times are simulated.
768 devices in a mesh: lat: 48 (over z, x_lo, core), fld: 16 (over x_hi, y).
Axes of the slice: x: 4 (x_hi: 2, x_lo: 2; x = x_hi * 2 + x_lo), y: 8, z: 12, core: 2. Of those that a mesh axis runs over, the one named last changes fastest.
Arguments:
- spectral: bfloat16 [768, 2, 16, 72, 640], P('lat', None, 'fld'), may hold values from -6 to 6
- legendre: bfloat16 [768, 96, 640], P('lat'), may hold values from -0.0078125 to 0.0078125
- wave_slot: int32 [768], replicated, may hold values from 0 to 767, each once
- coupling_in: bfloat16 [1044, 16], replicated, may hold values from -1.5 to 1.5
- interaction: bfloat16 [1044, 1044], replicated, may hold values from -0.1875 to 0.1875
- bin_speed: float32 [1044], replicated, may hold values from 0.02 to 0.2
- momentum: float32 [1044], replicated, may hold values from -1 to 1
- wave_state: bfloat16 [1044, 98304], P(None, ('lat', 'fld')), may hold values from 0.099609375 to 1
- cell_index: int32 [98304], P('lat'), may hold values from 0 to 245759
- edge_source: int32 [393216], P(('lat', 'fld')), may hold values from 0 to 255
- edge_target: int32 [393216], P(('lat', 'fld')), may hold values from 0 to 127
- surface_drag: float32 [16], P('fld'), may hold values from -4 to 4
- mixing: float32 [72], replicated, may hold values from 0.05 to 2
Outputs:
- mixed: bfloat16 [96, 16, 72, 2560], P('lat', 'fld')
- wave_next: bfloat16 [1044, 98304], P(None, ('lat', 'fld'))
Inputs may be any that keep to these rules, and one draw needn't show every extreme that they name: `wave_slot`: each slot holds a different wavenumber. `edge_source`: values below 64 name the previous tile's last points, values from 192 on the next tile's first points.
All inputs are finite; a program needn't handle non-finite values.
Results may differ from a plain program's by a relative error of at most 0.0085.
Values may be sent and summed in bfloat16 or wider, within the bound.
No kernel may reach another device: no remote copies, remote signals or barrier semaphores. Data moves between devices by JAX's collectives and lax.ppermute only.
A program may use at most 64 MiB of HBM per device.

v0:
```python
import jax
import jax.numpy as jnp
from jax import lax
from jax.sharding import PartitionSpec as P

LON = 2560
RIM = 64


time_step = 0.25


def in_order(parts, dim):
    lengths = list(parts.shape[1:])
    lengths[dim] *= parts.shape[0]
    return jnp.moveaxis(parts, 0, dim).reshape(lengths)


def sent_to_all(value, axis):
    copies = jnp.broadcast_to(value, (lax.axis_size(axis), *value.shape))
    return lax.all_to_all(copies, axis, split_axis=0, concat_axis=0, tiled=True)


def collect(value, axis, dim):
    return in_order(sent_to_all(value, axis), dim)


def extended_2(value, sides, width):
    edges = {}
    for axis, dim in sides:
        count, length = (lax.axis_size(axis), value.shape[dim])
        up = [(i, (i + 1) % count) for i in range(count - 1)]
        last = lax.slice_in_dim(value, length - width, length, axis=dim)
        initial = lax.slice_in_dim(value, 0, width, axis=dim)
        edges[dim] = (
            lax.ppermute(last, axis, up),
            lax.ppermute(initial, axis, [(b, a) for a, b in up]),
        )
    done = []
    for _, dim in sides:
        low, high = edges[dim]
        around = [(width, width) if d in done else (0, 0) for d in range(value.ndim)]
        value = jnp.concatenate([jnp.pad(low, around), value, jnp.pad(high, around)], axis=dim)
        done.append(dim)
    return value


def wave_angles(wave_slot, longitudes):
    column = jnp.arange(longitudes, dtype=jnp.int32)
    phases = (wave_slot[:, None] * column[None, :] % longitudes).astype(jnp.float32)
    angles = phases * (2.0 * jnp.pi / longitudes)
    return jnp.stack([jnp.cos(angles), -jnp.sin(angles)], axis=1).astype(jnp.bfloat16)


def local(
    spectral,
    legendre,
    wave_slot,
    coupling_in,
    interaction,
    bin_speed,
    momentum,
    wave_state,
    cell_index,
    edge_source,
    edge_target,
    surface_drag,
    mixing,
):
    slot_count = spectral.shape[0]
    degrees = spectral.shape[4]
    all_slots = wave_slot.shape[0]
    longitudes = LON
    own_slots = lax.dynamic_slice_in_dim(wave_slot, lax.axis_index("lat") * slot_count, slot_count)
    limits = degrees - own_slots * degrees // all_slots
    live_mask = (jnp.arange(degrees, dtype=jnp.int32)[None, :] < limits[:, None]).astype(
        jnp.bfloat16
    )
    masked = spectral * live_mask[:, None, None, None, :]
    fourier = jnp.einsum(
        "stn,scfln->tscfl", legendre, masked, preferred_element_type=jnp.float32
    ).astype(jnp.bfloat16)
    wave_table = wave_angles(wave_slot, longitudes)
    grid_rows = jnp.einsum(
        "tscfl,scj->tflj",
        lax.all_to_all(fourier, "lat", split_axis=0, concat_axis=1, tiled=True),
        wave_table,
        preferred_element_type=jnp.float32,
    ).astype(jnp.bfloat16)
    lat_rows = grid_rows.shape[0]
    field_count = grid_rows.shape[1]
    levels = grid_rows.shape[2]
    lowest = (
        grid_rows[:, :, levels - 1, :]
        .transpose(1, 0, 2)
        .reshape(field_count, lat_rows * longitudes)
    )
    surface = collect(lowest, "lat", 1)
    point_count = wave_state.shape[1]
    picked = surface[:, cell_index]
    forcing = lax.all_to_all(picked, "fld", split_axis=1, concat_axis=0, tiled=True)
    growth = jnp.tanh(jnp.dot(coupling_in, forcing, preferred_element_type=jnp.float32))
    extended = extended_2(wave_state, ((("lat", "fld"), 1),), RIM)
    extended_width = extended.shape[1]
    source_hot = (
        edge_source[:, None] == jnp.arange(extended_width, dtype=jnp.int32)[None, :]
    ).astype(jnp.float32)
    target_hot = (edge_target[:, None] == jnp.arange(point_count, dtype=jnp.int32)[None, :]).astype(
        jnp.float32
    )
    routes = jnp.dot(source_hot.T, target_hot, precision=lax.Precision.HIGHEST)
    counts = jnp.sum(target_hot, axis=0)
    inflow = jnp.dot(extended, routes.astype(jnp.bfloat16), preferred_element_type=jnp.float32)
    current = wave_state.astype(jnp.float32)
    advected = current + bin_speed[:, None] * (inflow - counts[None, :] * current)
    squared = (advected * advected).astype(jnp.bfloat16)
    transfer = jnp.dot(interaction, squared, preferred_element_type=jnp.float32)
    wave_new = advected + time_step * (growth * advected + transfer)
    stress = jnp.sum(momentum[:, None] * growth * wave_new, axis=0)
    cell_total = surface.shape[1]
    row_cells = lat_rows * longitudes
    own_cells = lax.dynamic_slice_in_dim(
        cell_index, lax.axis_index("fld") * point_count, point_count
    )
    partial_sum = jnp.zeros((cell_total,), jnp.float32).at[own_cells].add(stress)
    summed = lax.psum(partial_sum, ("lat", "fld"))
    stress_rows = lax.dynamic_slice_in_dim(summed, lax.axis_index("lat") * row_cells, row_cells)
    surface_push = stress_rows.reshape(lat_rows, 1, longitudes) * surface_drag[None, :, None]
    right_side = grid_rows.astype(jnp.float32)
    right_side = right_side.at[:, :, levels - 1, :].add(surface_push)
    zero_one = jnp.zeros((1,), jnp.float32)
    upper_band = jnp.concatenate([-mixing[:-1], zero_one])
    lower_band = jnp.concatenate([zero_one, -mixing[:-1]])
    middle = 1.0 + mixing + jnp.concatenate([zero_one, mixing[:-1]])
    column_batch = lat_rows * field_count
    solve_shape = (column_batch, levels)
    solved = lax.linalg.tridiagonal_solve(
        jnp.broadcast_to(lower_band, solve_shape),
        jnp.broadcast_to(middle, solve_shape),
        jnp.broadcast_to(upper_band, solve_shape),
        right_side.reshape(column_batch, levels, longitudes),
    )
    mixed = solved.reshape(lat_rows, field_count, levels, longitudes).astype(jnp.bfloat16)
    return (mixed, wave_new.astype(jnp.bfloat16))


def solution(mesh):
    in_specs = (
        P("lat", None, "fld", None, None),
        P("lat", None, None),
        P(),
        P(),
        P(),
        P(),
        P(),
        P(None, ("lat", "fld")),
        P("lat"),
        P(("lat", "fld")),
        P(("lat", "fld")),
        P("fld"),
        P(),
    )
    out_specs = (P("lat", "fld", None, None), P(None, ("lat", "fld")))
    return jax.shard_map(local, mesh=mesh, in_specs=in_specs, out_specs=out_specs, check_vma=False)
```

profile of v0, /device:TPU:1, one launch (start us, length us, event | category | flops | bytes accessed | tf_op | source)
XLA Modules:
  0.0 718.7 jit_solution(11216482818649117430)
XLA Ops:
  7.2 0.9 fusion.354
  8.2 3.5 fusion.314
  11.7 2.4 copy.392
  14.1 17.9 %all-to-all-start = ((bf16[96,16,2,1,72]{4,2,1,3,0:T(2,128)(2,1)}), bf16[96,16,2,1,72]{4,2,1,3,0:T(2,128)(2,1)S(1)}, u32[]{:S(2)}, u32[]{:S(2)}) async-start(bf16[96,16,2,1,72]{4,2,1,3,0:T(2,128)(2,1)} %copy.392), calls=%async_computation | async-start | bytes 1572864 | tf_op jit(solution)/shard_map/all_to_all | solution.py:86
  32.0 35.1 %cosine_convert_fusion = (bf16[768,1,2560]{2,0,1:T(8,128)(2,1)}, bf16[768,1,2560]{2,0,1:T(8,128)(2,1)}) fusion(s32[768]{0:T(1024)S(1)} %copy-done.8), kind=kLoop, calls=%fused_computation.588 | loop fusion | flops 23592960 | bytes 7867392 | tf_op jit(solution)/shard_map/convert.21
  67.4 5.9 fusion.481
  74.5 4.5 reduce.19
  79.0 2.2 reshape.855
  81.3 11.0 %all-to-all-start.1 = ((bf16[48,2,2560]{2,1,0:T(2,128)(2,1)}), bf16[48,2,2560]{2,1,0:T(2,128)(2,1)}, u32[]{:S(2)}, u32[]{:S(2)}) async-start(bf16[48,2,2560]{2,1,0:T(2,128)(2,1)} %reshape.855), calls=%async_computation.1 | async-start | bytes 983040 | tf_op jit(solution)/shard_map/all_to_all | solution.py:21
  93.2 3.2 collective-permute-start
  96.4 6.5 collective-permute-start.1
  103.8 12.7 %all-to-all-done.1 = bf16[48,2,2560]{2,1,0:T(2,128)(2,1)} async-done(((bf16[48,2,2560]{2,1,0:T(2,128)(2,1)}), bf16[48,2,2560]{2,1,0:T(2,128)(2,1)}, u32[]{:S(2)}, u32[]{:S(2)}) %all-to-all-start.1) | async-done | bytes 491552 | tf_op jit(solution)/shard_map/all_to_all | solution.py:21
  116.5 2.1 reshape.856
  118.6 3.9 reduce.3
  122.5 1.1 copy.472
  123.6 13.0 %gather_fusion = bf16[2048]{0:T(1024)(128)(2,1)S(1)} fusion(bf16[245760]{0:T(1024)(128)(2,1)S(1)} %bitcast.1837, s32[2048]{0:T(1024)S(1)} %fusion.351), kind=kCustom, calls=%fused_computation | custom fusion | bytes 16384 | tf_op jit(solution)/shard_map/gather | solution.py:100
  137.3 9.1 %all-to-all-start.2 = ((bf16[1,16,128]{2,0,1:T(2,128)(2,1)}), bf16[1,16,128]{2,0,1:T(2,128)(2,1)S(1)}, u32[]{:S(2)}, u32[]{:S(2)}) async-start(bf16[1,16,128]{2,0,1:T(2,128)(2,1)} %copy.396), calls=%async_computation.2 | async-start | bytes 16384 | tf_op jit(solution)/shard_map/all_to_all | solution.py:101
  146.5 2.3 fusion.302
  148.7 6.4 all-to-all-done.2
  155.6 2.9 fusion.475
  158.5 2.2 scatter_custom_fusion
  164.7 452.7 %all-reduce.2.cloned.1.call-done = f32[245760]{0:T(1024)} async-done(((f32[245760]{0:T(1024)}), f32[245760]{0:T(1024)}) %all-reduce.2.cloned.1.call-update) | async-done | bytes 983056 | tf_op jit(solution)/shard_map/psum | solution.py:126
  618.1 0.9 slice_add_fusion
  619.0 1.6 scatter-add.13
  620.7 1.6 slice_divide_fusion
  622.2 1.5 slice_bitcast_fusion
  623.8 1.1 slice.1508
  625.2 26.3 %while.35 = (s32[]{:T(128)}, f32[2]{0:T(128)S(1)}, f32[2,2560]{1,0:T(2,128)S(1)}, f32[2,32,2]{1,0,2:T(2,128)S(1)}, f32[2,32,2,2560]{3,2,1,0:T(2,128)}, /*index=5...) while((s32[]{:T(128)}, f32[2]{0:T(128)S(1)}, ...), condition=%wide.region_5.6_spmd.clone, body=%wide.region_4.5_spmd.sunk.clone | while | flops 737505 | bytes 15800317 | solution.py:137
  626.1 2.5 constant_dynamic-slice_fusion.165
  630.3 2.4 constant_dynamic-slice_fusion.164
  634.2 1.0 copy-done.2
  639.1 2.8 constant_dynamic-slice_fusion.165
  643.5 2.5 constant_dynamic-slice_fusion.164
  647.6 1.0 copy-done.2
  651.6 8.6 %multiply_subtract_fusion = (f32[2]{0:T(128)S(1)}, f32[2]{0:T(128)S(1)}, f32[2]{0:T(128)S(1)}, f32[2]{0:T(128)S(1)}, f32[2]{0:T(128)S(1)}, /*index=5*/f32[2]{0:T...) fusion(f32[]{:T(128)} %bitcast.321, ...), kind=kLoop, calls=%fused_computation.701 | loop fusion | flops 40 | bytes 168 | tf_op jit(solution)/shard_map/vmap()/eval_jaxpr/sub | solution.py:137
  661.5 1.4 constant_dynamic-update-slice_fusion.64
  663.6 1.4 bitcast_dynamic-update-slice_fusion.6
  665.7 1.3 bitcast_dynamic-update-slice_fusion.4
  667.0 1.9 bitcast_dynamic-update-slice_fusion.3
  669.5 1.1 slice.1523
  670.6 1.3 fusion.348
  671.9 32.4 %while.36 = (s32[]{:T(128)}, f32[2,2560]{1,0:T(2,128)S(1)}, bf16[2,32,2,2560]{3,2,1,0:T(2,128)(2,1)S(1)}, f32[2,32,2,2560]{3,2,1,0:T(2,128)}, f32[2,32,2]{2,1,0:T(8,128)S(1)}) while((s32[]{:T(128)}, f32[2,2560]{1,0:T(2,128)S(1)}, bf16[2,32,2,2560]{3,2,1,0:T(2,128)(2,1)S(1)}, f32[2,32,2,2560]{3,2,1,0:T(2,128)}, ...), condition=%wide.region_7.8_spmd.clone, body=%wide.region_6.7_spmd.sunk.clone | while | flops 501793 | bytes 3328077 | solution.py:137
  672.1 1.4 constant_dynamic-update-slice_fusion.225
  688.3 1.4 constant_dynamic-update-slice_fusion.225
  704.3 0.9 copy.413
  705.2 1.0 fusion.350
  706.5 4.3 concatenate.55
  710.8 1.1 pad_maximum_fusion
  (303 shorter events, 54.2 us)
Async XLA Ops:
  7.2 148.4 %copy-start = (bf16[1044,1044]{1,0:T(8,128)(2,1)S(1)}, bf16[1044,1044]{1,0:T(8,128)(2,1)}, u32[]{:S(2)}) copy-start(bf16[1044,1044]{1,0:T(8,128)(2,1)} %param.23) | copy-start | bytes 6539620
  11.7 20.3 %copy-start.8 = (s32[768]{0:T(1024)S(1)}, s32[768]{0:T(1024)}, u32[]{:S(2)}) copy-start(s32[768]{0:T(1024)} %param.21) | copy-start | bytes 9220
  14.1 53.1 %all-to-all-start = ((bf16[96,16,2,1,72]{4,2,1,3,0:T(2,128)(2,1)}), bf16[96,16,2,1,72]{4,2,1,3,0:T(2,128)(2,1)S(1)}, u32[]{:S(2)}, u32[]{:S(2)}) async-start(bf16[96,16,2,1,72]{4,2,1,3,0:T(2,128)(2,1)} %copy.392), calls=%async_computation | async-start | bytes 1572864 | tf_op jit(solution)/shard_map/all_to_all | solution.py:86
  79.0 13.3 %copy-start.3 = (bf16[1044,128]{1,0:T(8,128)(2,1)S(1)}, bf16[1044,128]{1,0:T(8,128)(2,1)}, u32[]{:S(2)}) copy-start(bf16[1044,128]{1,0:T(8,128)(2,1)} %param.26) | copy-start | bytes 801796
  79.0 23.8 %copy-start.10 = (f32[72]{0:T(128)S(1)}, f32[72]{0:T(128)}, u32[]{:S(2)}) copy-start(f32[72]{0:T(128)} %param.31) | copy-start | bytes 868
  79.0 24.0 %copy-start.7 = (s32[2048]{0:T(1024)S(1)}, s32[2048]{0:T(1024)}, u32[]{:S(2)}) copy-start(s32[2048]{0:T(1024)} %param.27) | copy-start | bytes 24580
  79.0 24.0 %copy-start.9 = (s32[512]{0:T(512)S(1)}, s32[512]{0:T(512)}, u32[]{:S(2)}) copy-start(s32[512]{0:T(512)} %param.29) | copy-start | bytes 6148
  79.0 24.0 %copy-start.12 = (s32[512]{0:T(512)S(1)}, s32[512]{0:T(512)}, u32[]{:S(2)}) copy-start(s32[512]{0:T(512)} %param.28) | copy-start | bytes 6148
  81.3 35.2 %all-to-all-start.1 = ((bf16[48,2,2560]{2,1,0:T(2,128)(2,1)}), bf16[48,2,2560]{2,1,0:T(2,128)(2,1)}, u32[]{:S(2)}, u32[]{:S(2)}) async-start(bf16[48,2,2560]{2,1,0:T(2,128)(2,1)} %reshape.855), calls=%async_computation.1 | async-start | bytes 983040 | tf_op jit(solution)/shard_map/all_to_all | solution.py:21
  93.2 53.2 %collective-permute-start = (bf16[1044,64]{1,0:T(8,128)(2,1)}, bf16[1044,64]{1,0:T(8,128)(2,1)}, u32[]{:S(2)}, u32[]{:S(2)}) collective-permute-start(bf16[1044,64]{1,0:T(8,128)(2,1)} %get-tuple-element.602), channel_id=1, source_target_pairs={{0,1},{1,2},{2,3},{3,4},{4,5},{5,6},{6,7},{7,8},{8,9},{9,10},{10,1... | collective-permute-start | bytes 400904 | tf_op jit(solution)/shard_map/ppermute | solution.py:36
  96.4 50.0 %collective-permute-start.1 = (bf16[1044,64]{1,0:T(8,128)(2,1)}, bf16[1044,64]{1,0:T(8,128)(2,1)}, u32[]{:S(2)}, u32[]{:S(2)}) collective-permute-start(bf16[1044,64]{1,0:T(8,128)(2,1)} %get-tuple-element.603), channel_id=1, source_target_pairs={{1,0},{2,1},{3,2},{4,3},{5,4},{6,5},{7,6},{8,7},{9,8},{10,9},{11,1... | collective-permute-start | bytes 400904 | tf_op jit(solution)/shard_map/ppermute | solution.py:37
  123.6 22.9 %copy-start.4 = (bf16[1044,128]{1,0:T(8,128)(2,1)S(1)}, bf16[1044,128]{1,0:T(8,128)(2,1)}, u32[]{:S(2)}) copy-start(bf16[1044,128]{1,0:T(8,128)(2,1)} %param.26) | copy-start | bytes 801796
  123.6 22.9 %copy-start.11 = (f32[1044]{0:T(1024)S(1)}, f32[1044]{0:T(1024)}, u32[]{:S(2)}) copy-start(f32[1044]{0:T(1024)} %param.24) | copy-start | bytes 12532
  136.6 18.5 %copy-start.5 = (bf16[1044,16]{0,1:T(8,128)(2,1)S(1)}, bf16[1044,16]{0,1:T(8,128)(2,1)}, u32[]{:S(2)}) copy-start(bf16[1044,16]{0,1:T(8,128)(2,1)} %param.22) | copy-start | bytes 100228
  136.6 18.9 %copy-start.6 = (f32[1044]{0:T(1024)S(1)}, f32[1044]{0:T(1024)}, u32[]{:S(2)}) copy-start(f32[1044]{0:T(1024)} %param.25) | copy-start | bytes 12532
  137.3 17.9 %all-to-all-start.2 = ((bf16[1,16,128]{2,0,1:T(2,128)(2,1)}), bf16[1,16,128]{2,0,1:T(2,128)(2,1)S(1)}, u32[]{:S(2)}, u32[]{:S(2)}) async-start(bf16[1,16,128]{2,0,1:T(2,128)(2,1)} %copy.396), calls=%async_computation.2 | async-start | bytes 16384 | tf_op jit(solution)/shard_map/all_to_all | solution.py:101
  146.4 471.0 %all-reduce.2.cloned.1.call-start = ((), (), s32[]{:S(2)}) async-start(), calls=%async_computation.3 | async-start | bytes 1966080 | tf_op jit(solution)/shard_map/psum | solution.py:126
  629.1 4.9 copy-start.1
  634.1 1.1 copy-start.2
  642.3 5.0 copy-start.1
  647.5 1.1 copy-start.2
Sparse Core Ops, SparseCore 0:
  160.8 456.4 all-reduce.1
where the time goes:
time: 722 us; the launch traced here: 719 us
  waiting for transfers between devices  472 us (65%)
  other arithmetic  107 us (15%)
  local copies, waits for them, and re-layouts  59.4 us (8%)
  starting transfers between devices  47.7 us (7%)
  between operations  16.5 us (2%)
  matrix products  15.5 us (2%)
    psum x1, waiting for transfers between devices, local(): summed = lax.psum(partial_sum, ('lat', 'fld'))  453 us
    another operation x2, other arithmetic  35.1 us
    while x94, other arithmetic  35.1 us
    all_to_all x1, starting transfers between devices, local(): lax.all_to_all(fourier, 'lat', split_axis=0, concat_axis=1, tiled=True)  17.9 us
  transfers between devices with their start and end apart: 6, of which 3 were waited for; matrix products, arithmetic and copies ran while one was open for 9% of the time, Pallas kernels for 0%

commit v1 on v0

v1 whole, which is shorter than its diff:
```python
import functools

import jax
import jax.numpy as jnp
from jax import lax
from jax.experimental import pallas as pl
from jax.experimental.pallas import tpu as pltpu
from jax.sharding import PartitionSpec as P

LON = 2560
RIM = 64
QUARTER = LON // 4
LANES = 128

time_step = 0.25

bf16 = jnp.bfloat16
f32 = jnp.float32
i32 = jnp.int32

NN = (((1,), (0,)), ((), ()))
NT = (((1,), (1,)), ((), ()))

VMEM = pl.BlockSpec(memory_space=pltpu.VMEM)
SMEM = pl.BlockSpec(memory_space=pltpu.SMEM)


def dot(a, b, dims=NN):
    return lax.dot_general(a, b, dims, preferred_element_type=f32)


def lane_of(shape):
    return lax.broadcasted_iota(i32, shape, len(shape) - 1)


def params(mib, **more):
    return pltpu.CompilerParams(vmem_limit_bytes=mib << 20, **more)


def cost(flops, nbytes, trans=0):
    return pl.CostEstimate(flops=int(flops), bytes_accessed=int(nbytes), transcendentals=int(trans))


def legendre_kernel(per, slots, lats, levels, limit_ref, leg_ref, spec_ref, f0_ref, f1_ref, x_ref, s0, s1, low):
    step = pl.program_id(0)

    @pl.when(step == 0)
    def _():
        low[...] = jnp.zeros_like(low)

    degrees = leg_ref.shape[2]
    column = lane_of((1, degrees))
    lane = lane_of((lats, LANES))
    picked = low[0:lats, :]
    fill = jnp.zeros((lats, LANES - levels), f32)
    for k in range(per):
        slot = step * per + k
        live = column < limit_ref[slot]
        weights = jnp.where(live, leg_ref[k].astype(f32), 0.0).astype(bf16)
        for c, store in ((0, s0), (1, s1)):
            sums = dot(weights, spec_ref[k, c, 0], NT)
            store[pl.ds(slot, lats, stride=slots), :] = jnp.concatenate([sums, fill], axis=1)
            lowest = jnp.broadcast_to(sums[:, levels - 1 : levels], (lats, LANES))
            picked = jnp.where(lane == c * slots + slot, lowest, picked)
    low[0:lats, :] = picked

    @pl.when(step == pl.num_programs(0) - 1)
    def _():
        f0_ref[...] = s0[:, 0:levels].astype(bf16)
        f1_ref[...] = s1[:, 0:levels].astype(bf16)
        turned = low[...].T
        tail = turned[24:32, :]
        lane8 = lane_of((8, LANES))
        rows = [
            jnp.where(lane8 < 96, turned[8 * h : 8 * h + 8, :], pltpu.roll(tail, 96 - 32 * h, 1))
            for h in range(3)
        ]
        packed = jnp.concatenate(rows, axis=0).astype(bf16)
        x_ref[...] = jnp.broadcast_to(packed[None], x_ref.shape)


def inverse_kernel(levels, mix_ref, w_ref, col_ref, left, right):
    width = 2 * LANES
    lane = lax.broadcasted_iota(i32, (2, width), 1)
    start = lax.broadcasted_iota(i32, (2, width), 0) * levels
    unit = lane - start
    ratio, part = [], []
    for level in range(levels):
        below = jnp.full((2, width), mix_ref[level], f32)
        rhs = (unit == level).astype(f32)
        if level == 0:
            scale = 1.0 / (1.0 + below)
            part.append(rhs * scale)
        else:
            above = jnp.full((2, width), mix_ref[level - 1], f32)
            scale = 1.0 / (1.0 + below + above - above * ratio[-1])
            part.append((rhs + above * part[-1]) * scale)
        ratio.append(below * scale)
    solved = part[-1]
    for level in range(levels - 1, -1, -1):
        if level < levels - 1:
            solved = part[level] + ratio[level] * solved
        left[2 * level : 2 * level + 2, :] = solved[:, :LANES]
        right[2 * level : 2 * level + 2, :] = solved[:, LANES:]
    for c in range(2):
        block = jnp.concatenate([half[pl.ds(c, levels, stride=2), :] for half in (left, right)], axis=1)
        high = block.astype(bf16)
        w_ref[2 * c] = high
        w_ref[2 * c + 1] = (block - high.astype(f32)).astype(bf16)
        if c == 0:
            col_ref[...] = jnp.broadcast_to(block[:, levels - 1 : levels], col_ref.shape)


def mix_kernel(owners, f0_ref, f1_ref, w_ref, codes_ref, o_ref, rest):
    sums = dot(f0_ref[...], w_ref[0]) + dot(f0_ref[...], w_ref[1])
    sums += dot(f1_ref[...], w_ref[2]) + dot(f1_ref[...], w_ref[3])
    count = sums.shape[0]
    rest[...] = sums[:, LANES:]
    lane = lane_of((count // 4, LANES))
    tail = jnp.broadcast_to(codes_ref[...][None], (owners, 8, LANES)).reshape(count // 4, LANES)
    for g in range(4):
        piece = rest[pl.ds(g, count // 4, stride=4), :]
        if g:
            piece = pltpu.roll(piece, 16 * g, 1)
        tail = jnp.where((lane >= 16 * g) & (lane < 16 * g + 16), piece, tail)
    whole = jnp.concatenate(
        [sums[:, :LANES].reshape(owners, count // owners, LANES), tail.reshape(owners, 8, LANES)], axis=1
    )
    o_ref[...] = whole.astype(bf16)


def table_kernel(slots, bc_ref, bs_ref, ac_ref, as_ref, cc_ref, cs_ref, long_ref, wide_ref):
    bc, bs = bc_ref[...], bs_ref[...]
    for a in range(QUARTER // LANES):
        ca, sa = ac_ref[a : a + 1, :], as_ref[a : a + 1, :]
        rows = slice(a * LANES, (a + 1) * LANES)
        long_ref[rows, 0:slots] = (ca * bc - sa * bs).astype(bf16)
        long_ref[rows, slots : 2 * slots] = (-(sa * bc + ca * bs)).astype(bf16)
    for first in range(0, slots, LANES):
        mine = slice(first, first + LANES)
        tc, ts = bc[:, mine].T, bs[:, mine].T
        for a in range(QUARTER // LANES):
            ca, sa = cc_ref[mine, a : a + 1], cs_ref[mine, a : a + 1]
            columns = slice(a * LANES, (a + 1) * LANES)
            wide_ref[mine, columns] = (ca * tc - sa * ts).astype(bf16)
            wide_ref[slots + first : slots + first + LANES, columns] = (-(sa * tc + ca * ts)).astype(bf16)


def turned_pair(first, second, wave, m):
    if m == 0:
        return first, second
    turns = (wave * m) & 3
    even = (turns & 1) == 0
    sign0 = jnp.where((turns == 0) | (turns == 3), 1.0, -1.0)
    sign1 = jnp.where((turns == 0) | (turns == 1), 1.0, -1.0)
    return jnp.where(even, first, second) * sign0, jnp.where(even, second, first) * sign1


def surface_kernel(slots, x_ref, long_ref, wave_ref, row_ref, hot_ref, o_ref, surface, picked):
    peers = x_ref.shape[0]
    x = x_ref[...].astype(f32)
    lane = lane_of((peers, 8, LANES))
    tail = jnp.zeros((peers, 8, LANES), f32)
    for h in range(3):
        moved = pltpu.roll(x[:, 8 * h : 8 * h + 8, :].reshape(peers * 8, LANES), 32 + 32 * h, 1)
        tail = jnp.where((lane >= 32 * h) & (lane < 32 * h + 32), moved.reshape(peers, 8, LANES), tail)
    real = x[:, 0:16, :].reshape(slots, LANES)
    imaginary = jnp.concatenate([x[:, 16:24, :], tail], axis=1).reshape(slots, LANES)
    wave = jnp.broadcast_to(wave_ref[...], (slots, LANES))
    pairs = [turned_pair(real, imaginary, wave, m) for m in range(4)]
    coefficients = jnp.concatenate(
        [jnp.concatenate([p[c].astype(bf16) for p in pairs], axis=1) for c in range(2)], axis=0
    )
    values = dot(long_ref[...], coefficients).astype(bf16).astype(f32)
    for m in range(4):
        surface[m * QUARTER : (m + 1) * QUARTER, :] = values[:, m * LANES : (m + 1) * LANES]

    def fetch(block, carry):
        for u in range(32):
            p = block * 32 + u
            picked[pl.ds(p, 1), :] = surface[pl.ds(row_ref[p], 1), :]
        return carry

    points = hot_ref.shape[0]
    lax.fori_loop(0, points // 32, fetch, 0)
    chosen = (picked[...] * hot_ref[...].astype(f32)).astype(bf16)
    lined = dot(jnp.ones((8, LANES), bf16), chosen, NT)
    rows = [lined[0:1, k * LANES : (k + 1) * LANES] for k in range(points // LANES)]
    o_ref[...] = jnp.concatenate(rows, axis=0).astype(bf16)


def advect_kernel(state_ref, rims_ref, source_ref, target_ref, speed_ref, inter_ref, adv_ref, base_ref):
    edges = source_ref.shape[1]
    points = state_ref.shape[1]
    source_hot = (lax.broadcasted_iota(i32, (points + 2 * RIM, edges), 0) == source_ref[...]).astype(f32)
    target_hot = (lax.broadcasted_iota(i32, (points, edges), 0) == target_ref[...]).astype(f32)
    source_hot, target_hot = source_hot.astype(bf16), target_hot.astype(bf16)
    routes = dot(source_hot, target_hot, NT)
    counts = dot(jnp.ones((8, edges), bf16), target_hot, NT)[0:1, :]
    rim_routes = jnp.concatenate([routes[0:RIM], routes[RIM + points :]], axis=0)
    own_routes = routes[RIM : RIM + points]
    inflow = None
    for values, table in ((state_ref[...], own_routes), (rims_ref[...], rim_routes)):
        high = table.astype(bf16)
        rest = (table - high.astype(f32)).astype(bf16)
        part = dot(values, high) + dot(values, rest)
        inflow = part if inflow is None else inflow + part
    current = state_ref[...].astype(f32)
    advected = current + speed_ref[...] * (inflow - counts * current)
    squared = (advected * advected).astype(bf16)
    transfer = dot(inter_ref[...], squared)
    adv_ref[...] = time_step * advected
    base_ref[...] = advected + time_step * transfer


def wave_kernel(forcing_ref, coupling_ref, adv_ref, base_ref, momentum_ref, next_ref, stress_ref):
    growth = jnp.tanh(dot(coupling_ref[...], forcing_ref[...]))
    wave_new = base_ref[...] + growth * adv_ref[...]
    next_ref[...] = wave_new.astype(bf16)
    stress = jnp.sum(momentum_ref[...] * growth * wave_new, axis=0, keepdims=True)
    stress_ref[...] = jnp.broadcast_to(stress, stress_ref.shape)


def synthesis_kernel(
    slots, levels, y_ref, wave_ref, wide_ref, base_ref, d_ref, high_ref, hot_ref, rest, tails, lhs
):
    peers = y_ref.shape[0]
    y = y_ref[...].astype(f32)
    main = y[:, 0:32, :]
    tail = y[:, 32:40, :].reshape(peers * 8, LANES)
    tails[...] = tail
    for g in range(4):
        rest[pl.ds(g, peers * 8, stride=4), :] = pltpu.roll(tail, LANES - 16 * g, 1) if g else tail
    wave = wave_ref[...]
    others = rest[...].reshape(peers, 32, LANES)
    padded = 80
    fill = jnp.zeros((padded - levels, slots), f32)
    for t in range(2):
        a = main[:, 16 * t : 16 * t + 16, :].reshape(slots, LANES).T
        b = others[:, 16 * t : 16 * t + 16, :].reshape(slots, LANES).T
        first = a[0:levels]
        second = jnp.concatenate([a[levels:], b[0 : 2 * levels - LANES]], axis=0)
        for m in range(4):
            p, q = turned_pair(first, second, wave, m)
            rows = slice((t * 4 + m) * padded, (t * 4 + m + 1) * padded)
            lhs[rows, 0:slots] = jnp.concatenate([p, fill], axis=0).astype(bf16)
            lhs[rows, slots : 2 * slots] = jnp.concatenate([q, fill], axis=0).astype(bf16)
    for t in range(2):
        sums = dot(lhs[t * 4 * padded : (t + 1) * 4 * padded, :], wide_ref[...])
        for m in range(4):
            d_ref[t, :, m * QUARTER : (m + 1) * QUARTER] = sums[m * padded : m * padded + levels]
    lane = lane_of((peers, LANES))
    parts = []
    for v in range(3):
        left = pltpu.roll(tails[pl.ds(2 * v, peers, stride=8), :], 64, 1)
        parts.append(jnp.where(lane < 64, left, tails[pl.ds(2 * v + 1, peers, stride=8), :]))
    cell = (parts[0] * 65536.0 + parts[1] * 256.0 + parts[2]).astype(i32) - base_ref[0]
    high_ref[...] = cell >> 7
    at = cell & (LANES - 1)
    row = lax.broadcasted_iota(i32, (LANES, LANES), 0)
    for k in range(peers):
        hot_ref[:, k * LANES : (k + 1) * LANES] = (row == at[k : k + 1, :]).astype(f32).astype(bf16)


def scatter_kernel(stress_ref, high_ref, hot_ref, o_ref):
    peers = stress_ref.shape[0]
    height = o_ref.shape[1]
    row = lax.broadcasted_iota(i32, (height, LANES), 0)
    first, second = [], []
    for k in range(peers):
        spread = jnp.where(row == high_ref[k : k + 1, :], stress_ref[k : k + 1, :], 0.0)
        high = spread.astype(bf16)
        first.append(high)
        second.append((spread - high.astype(f32)).astype(bf16))
    hot = hot_ref[...]
    sums = dot(jnp.concatenate(first, axis=1), hot, NT) + dot(jnp.concatenate(second, axis=1), hot, NT)
    o_ref[...] = jnp.broadcast_to(sums.astype(bf16)[None], o_ref.shape)


def final_kernel(d_ref, part_ref, col_ref, drag_ref, o_ref):
    stress = jnp.sum(part_ref[...].astype(f32), axis=0)
    push = col_ref[...] * drag_ref[0]
    chunks = LON // LANES
    for t in range(2):
        for k in range(chunks):
            columns = slice(k * LANES, (k + 1) * LANES)
            line = stress[t * chunks + k : t * chunks + k + 1, :]
            o_ref[t, 0, :, columns] = (d_ref[t, :, columns] + push * line).astype(bf16)


def local(
    spectral,
    legendre,
    wave_slot,
    coupling_in,
    interaction,
    bin_speed,
    momentum,
    wave_state,
    cell_index,
    edge_source,
    edge_target,
    surface_drag,
    mixing,
):
    slots, _, _, levels, degrees = spectral.shape
    lats = legendre.shape[1]
    all_slots = wave_slot.shape[0]
    owners = lax.axis_size("lat")
    columns = lax.axis_size("fld")
    bins, points = wave_state.shape
    lat, fld = lax.axis_index("lat"), lax.axis_index("fld")
    shape = jax.ShapeDtypeStruct

    own_slots = lax.dynamic_slice_in_dim(wave_slot, lat * slots, slots)
    limits = degrees - own_slots * degrees // all_slots
    per = 4
    f0, f1, lowest = pl.pallas_call(
        functools.partial(legendre_kernel, per, slots, lats, levels),
        grid=(slots // per,),
        in_specs=[
            SMEM,
            pl.BlockSpec((per, lats, degrees), lambda i: (i, 0, 0)),
            pl.BlockSpec((per, 2, 1, levels, degrees), lambda i: (i, 0, 0, 0, 0)),
        ],
        out_specs=[
            pl.BlockSpec((lats * slots, levels), lambda i: (0, 0)),
            pl.BlockSpec((lats * slots, levels), lambda i: (0, 0)),
            pl.BlockSpec((owners, 24, LANES), lambda i: (0, 0, 0)),
        ],
        out_shape=[
            shape((lats * slots, levels), bf16),
            shape((lats * slots, levels), bf16),
            shape((owners, 24, LANES), bf16),
        ],
        scratch_shapes=[
            pltpu.VMEM((lats * slots, LANES), f32),
            pltpu.VMEM((lats * slots, LANES), f32),
            pltpu.VMEM((LANES, LANES), f32),
        ],
        compiler_params=params(16),
        cost_estimate=cost(3e8, 5e6),
        name="legendre",
    )(limits, legendre, spectral)
    gathered = lax.all_to_all(lowest, "lat", split_axis=0, concat_axis=0, tiled=True)

    tiles = owners * columns
    up = [(k, k + 1) for k in range(tiles - 1)]
    low = lax.ppermute(wave_state[:, points - RIM :], ("lat", "fld"), up)
    high = lax.ppermute(wave_state[:, :RIM], ("lat", "fld"), [(b, a) for a, b in up])

    mixers, column = pl.pallas_call(
        functools.partial(inverse_kernel, levels),
        in_specs=[SMEM],
        out_specs=[VMEM, VMEM],
        out_shape=[shape((4, levels, 2 * LANES), bf16), shape((levels, LANES), f32)],
        scratch_shapes=[pltpu.VMEM((2 * levels, LANES), f32)] * 2,
        compiler_params=params(8),
        cost_estimate=cost(3e6, 2e5),
        name="inverse",
    )(mixing)
    own_cells = lax.dynamic_slice_in_dim(cell_index, fld * points, points)
    codes = jnp.stack([own_cells >> 16, (own_cells >> 8) & 255, own_cells & 255])
    codes = jnp.pad(codes.astype(f32).reshape(6, 64), ((0, 2), (64, 0)))
    packed = pl.pallas_call(
        functools.partial(mix_kernel, owners),
        in_specs=[VMEM] * 4,
        out_specs=VMEM,
        out_shape=shape((owners, 40, LANES), bf16),
        scratch_shapes=[pltpu.VMEM((lats * slots, LANES), f32)],
        compiler_params=params(16),
        cost_estimate=cost(2e8, 2e6),
        name="mix",
    )(f0, f1, mixers, codes)
    bulk = lax.all_to_all(packed, "lat", split_axis=0, concat_axis=0, tiled=True)

    def angles(steps):
        phase = (steps % LON).astype(f32) * (2.0 * jnp.pi / LON)
        return jnp.cos(phase), jnp.sin(phase)

    coarse = jnp.arange(8, dtype=i32) * LANES
    fine = jnp.concatenate([jnp.arange(LANES, dtype=i32), coarse])
    rows_cos, rows_sin = angles(fine[:, None] * wave_slot[None, :])
    cols_cos, cols_sin = angles(wave_slot[:, None] * coarse[None, :])
    long, wide = pl.pallas_call(
        functools.partial(table_kernel, all_slots),
        in_specs=[VMEM] * 6,
        out_specs=[VMEM, VMEM],
        out_shape=[shape((QUARTER, 2 * all_slots), bf16), shape((2 * all_slots, QUARTER), bf16)],
        compiler_params=params(16),
        cost_estimate=cost(6e6, 5e6),
        name="table",
    )(rows_cos[:LANES], rows_sin[:LANES], rows_cos[LANES:], rows_sin[LANES:], cols_cos, cols_sin)

    adv, base = pl.pallas_call(
        advect_kernel,
        in_specs=[VMEM] * 6,
        out_specs=[VMEM, VMEM],
        out_shape=[shape((bins, points), f32)] * 2,
        compiler_params=params(24),
        cost_estimate=cost(5e8, 4e6),
        name="advect",
    )(
        wave_state,
        jnp.concatenate([low, high], axis=1),
        edge_source[None, :],
        edge_target[None, :],
        bin_speed[:, None],
        interaction,
    )

    lat_row = cell_index // LON
    rows = cell_index - lat_row * LON
    hot = (lat_row[:, None] == jnp.arange(LANES, dtype=i32)[None, :]).astype(bf16)
    total_points = cell_index.shape[0]
    picked = pl.pallas_call(
        functools.partial(surface_kernel, all_slots),
        in_specs=[VMEM, VMEM, VMEM, SMEM, VMEM],
        out_specs=VMEM,
        out_shape=shape((columns, points), bf16),
        scratch_shapes=[pltpu.VMEM((LON, LANES), f32), pltpu.VMEM((total_points, LANES), f32)],
        compiler_params=params(32),
        cost_estimate=cost(1e9, 4e6),
        name="surface",
    )(gathered, long, wave_slot[:, None], rows, hot)
    forcing = lax.all_to_all(picked, "fld", split_axis=0, concat_axis=0, tiled=True)

    wave_next, stress = pl.pallas_call(
        wave_kernel,
        in_specs=[VMEM] * 5,
        out_specs=[VMEM, VMEM],
        out_shape=[shape((bins, points), bf16), shape((owners, points), f32)],
        compiler_params=params(16),
        cost_estimate=cost(1e7, 2e6, bins * points),
        name="wave",
    )(forcing, coupling_in, adv, base, momentum[:, None])
    stresses = lax.all_to_all(stress, "lat", split_axis=0, concat_axis=0, tiled=True)

    bulk, _ = lax.optimization_barrier((bulk, stress))
    lat_rows = lats // owners
    row_cells = lat_rows * LON
    mixed_rows, place_high, place_hot = pl.pallas_call(
        functools.partial(synthesis_kernel, all_slots, levels),
        in_specs=[VMEM, VMEM, VMEM, SMEM],
        out_specs=[VMEM, VMEM, VMEM],
        out_shape=[
            shape((lat_rows, levels, LON), f32),
            shape((owners, points), i32),
            shape((LANES, owners * points), bf16),
        ],
        scratch_shapes=[
            pltpu.VMEM((owners * 32, LANES), f32),
            pltpu.VMEM((owners * 8, LANES), f32),
            pltpu.VMEM((640, 2 * all_slots), bf16),
        ],
        compiler_params=params(32),
        cost_estimate=cost(1.2e9, 6e6),
        name="synthesis",
    )(bulk, wave_slot[None, :], wide, (lat * row_cells)[None])

    partial = pl.pallas_call(
        scatter_kernel,
        in_specs=[VMEM] * 3,
        out_specs=VMEM,
        out_shape=shape((columns, row_cells // LANES, LANES), bf16),
        compiler_params=params(16),
        cost_estimate=cost(1e8, 2e6),
        name="scatter",
    )(stresses, place_high, place_hot)
    partials = lax.all_to_all(partial, "fld", split_axis=0, concat_axis=0, tiled=True)

    mixed = pl.pallas_call(
        final_kernel,
        in_specs=[VMEM, VMEM, VMEM, SMEM],
        out_specs=VMEM,
        out_shape=shape((lat_rows, 1, levels, LON), bf16),
        compiler_params=params(16),
        cost_estimate=cost(1e6, 3e6),
        name="final",
    )(mixed_rows, partials, column, surface_drag)
    return (mixed, wave_next)


def solution(mesh):
    in_specs = (
        P("lat", None, "fld", None, None),
        P("lat", None, None),
        P(),
        P(),
        P(),
        P(),
        P(),
        P(None, ("lat", "fld")),
        P("lat"),
        P(("lat", "fld")),
        P(("lat", "fld")),
        P("fld"),
        P(),
    )
    out_specs = (P("lat", "fld", None, None), P(None, ("lat", "fld")))
    return jax.shard_map(local, mesh=mesh, in_specs=in_specs, out_specs=out_specs, check_vma=False)
```

time: 722 us -> 141 us (0.20)
  waiting for transfers between devices: 472 us -> 39.2 us
  other arithmetic: 107 us -> 5.66 us
  local copies, waits for them, and re-layouts: 59.4 us -> 14.2 us
  Pallas kernels: 0 us -> 22.1 us
  matrix products: 15.5 us -> 0 us
  between operations: 16.5 us -> 1.62 us
  starting transfers between devices: 47.7 us -> 56.8 us
    psum x1 -> x0, waiting for transfers between devices: 453 us -> none  [local(): summed = lax.psum(partial_sum, ('lat', 'fld'))]
    another operation x2 -> x1, other arithmetic: 35.1 us -> 0.08 us  [local(): codes = jnp.stack([own_cells >> 16, own_cells >> 8 & 255, own_cells & 255])]
    while x94 -> x0, other arithmetic: 35.1 us -> none
    pallas_call x0 -> x10, Pallas kernels: none -> 22.1 us  [the longest x1 4.3 us: local(): pl.pallas_call(functools.partial(surface_kernel, all_slots), in_specs=[VM...]
    dot_general x6 -> x0, matrix products: 15.5 us -> none  [the longest x1 5.95 us: local(): jnp.einsum('tscfl,scj->tflj', lax.all_to_all(fourier, 'lat', split_axis=0...]
    slice x15 -> x5, local copies, waits for them, and re-layouts: 15.3 us -> 0.94 us  [the longest x1 0.88 us: local(): low = lax.ppermute(wave_state[:, points - RIM:], ('lat', 'fld'), up)]
    all_to_all x3 -> x5, starting transfers between devices: 38 us -> 51.4 us  [the longest x1 18.1 us: local(): lax.all_to_all(lowest, 'lat', split_axis=0, concat_axis=0, tiled=True)]
    gather x1 -> x0, local copies, waits for them, and re-layouts: 13 us -> none  [local(): picked = surface[:, cell_index]]
  transfers between devices with their start and end apart: 6 -> 7, of which waited for: 3 -> 7; matrix products, arithmetic and copies ran while one was open for 9% -> 6% of each run, Pallas kernels for 0% -> 8%
where the time goes in v1:
time: 141 us; the launch traced here: 140 us
  starting transfers between devices  56.8 us (40%)
  waiting for transfers between devices  39.2 us (28%)
  Pallas kernels  22.1 us (16%)
  local copies, waits for them, and re-layouts  14.2 us (10%)
  other arithmetic  5.66 us (4%)
  between operations  1.62 us (1%)
    all_to_all x1, starting transfers between devices, local(): lax.all_to_all(lowest, 'lat', split_axis=0, concat_axis=0, tiled=True)  18.1 us
    all_to_all x1, starting transfers between devices, local(): lax.all_to_all(stress, 'lat', split_axis=0, concat_axis=0, tiled=True)  11.4 us
    unnamed x34, local copies, waits for them, and re-layouts  10.3 us
    all_to_all x1, starting transfers between devices, local(): lax.all_to_all(picked, 'fld', split_axis=0, concat_axis=0, tiled=True)  9.09 us
    all_to_all x1, waiting for transfers between devices, local(): lax.all_to_all(partial, 'fld', split_axis=0, concat_axis=0, tiled=True)  8.31 us
    all_to_all x1, waiting for transfers between devices, local(): lax.all_to_all(lowest, 'lat', split_axis=0, concat_axis=0, tiled=True)  8.06 us
    ppermute x1, waiting for transfers between devices, local(): low = lax.ppermute(wave_state[:, points - RIM:], ('lat', 'fld'), up)  7.04 us
    all_to_all x1, waiting for transfers between devices, local(): lax.all_to_all(picked, 'fld', split_axis=0, concat_axis=0, tiled=True)  6.86 us
  transfers between devices with their start and end apart: 7, of which 7 were waited for; matrix products, arithmetic and copies ran while one was open for 6% of the time, Pallas kernels for 8%

profile of v1, /device:TPU:1, one launch (start us, length us, event | category | flops | bytes accessed | tf_op | source)
XLA Modules:
  0.0 139.6 jit_solution(8855975015148369271)
XLA Ops:
  0.6 0.8 fusion.13.limit_ref
  1.4 1.8 %copy-done = bf16[16,2,1,72,640]{4,3,2,1,0:T(8,128)(2,1)S(1)} copy-done((bf16[16,2,1,72,640]{4,3,2,1,0:T(8,128)(2,1)S(1)}, bf16[16,2,1,72,640]{4,3,2,1,0:T(8,128)(2,1)}, u32[]{:S(2)}) %copy-start) | copy-done | bytes 2949144
  3.3 1.5 %copy-done.4 = bf16[16,96,640]{2,1,0:T(8,128)(2,1)S(1)} copy-done((bf16[16,96,640]{2,1,0:T(8,128)(2,1)S(1)}, bf16[16,96,640]{2,1,0:T(8,128)(2,1)}, u32[]{:S(2)}) %copy-start.4) | copy-done | bytes 1966104
  4.8 3.7 %legendre.1 = (bf16[1536,72]{1,0:T(8,128)(2,1)S(1)}, bf16[1536,72]{1,0:T(8,128)(2,1)S(1)}, bf16[48,24,128]{2,1,0:T(8,128)(2,1)}) custom-call(s32[16]{0:T(128)S(1)} %fusion.13.limit_ref, bf16[16,96,640]{2,1,0:T(8,128)(2,1)S(1)} %copy-done.4, bf16[16,2,1,72,640]{4,3,2,1,0:T(8,128)(2,1)S(1)} %copy-done), custom_call_target="tpu_custom_call" | custom-call | flops 300000000 | bytes 5000000 | tf_op jit(solution)/shard_map/legendre/pallas_call | solution.py:318
  8.5 18.1 %all-to-all-start.1 = ((bf16[48,24,128]{2,1,0:T(8,128)(2,1)}), bf16[48,24,128]{2,1,0:T(8,128)(2,1)S(1)}, u32[]{:S(2)}, u32[]{:S(2)}) async-start(bf16[48,24,128]{2,1,0:T(8,128)(2,1)} %get-tuple-element.20), calls=%async_computation.1 | async-start | bytes 589824 | tf_op jit(solution)/shard_map/all_to_all | solution.py:345
  26.6 1.8 %fusion.5 = (f32[136,768]{1,0:T(8,128)S(1)}, f32[136,768]{1,0:T(8,128)S(1)}) fusion(s32[768]{0:T(1024)S(1)} %copy-done.12, s32[136]{0:T(256)S(1)} %pad_add_fusion), kind=kLoop, calls=%fused_computation.8 | loop fusion | flops 940032 | bytes 839200 | tf_op jit(solution)/shard_map/sin | solution.py:379
  28.4 0.1 fusion.8
  28.5 0.2 broadcast_in_dim.34.wave_ref
  28.7 1.4 %inverse.1 = (bf16[4,72,256]{2,1,0:T(8,128)(2,1)S(1)}, f32[72,128]{1,0:T(8,128)S(1)}) custom-call(f32[72]{0:T(128)S(1)} %copy-done.11), custom_call_target="tpu_custom_call" | custom-call | flops 3000000 | bytes 200000 | tf_op jit(solution)/shard_map/inverse/pallas_call | solution.py:352
  30.1 0.1 shift-right-arithmetic_bitcast_fusion
  30.2 0.1 convert_element_type.19
  30.3 0.2 copy.32
  30.5 0.1 pad.4.codes_ref
  30.5 1.4 %multiply_sine_fusion = (f32[768,8]{1,0:T(8,128)S(1)}, f32[768,8]{1,0:T(8,128)S(1)}) fusion(f32[768,8]{1,0:T(8,128)S(1)} %copy.32), kind=kLoop, calls=%fused_computation.11 | loop fusion | flops 6144 | bytes 73728 | tf_op jit(solution)/shard_map/sin | solution.py:379
  32.0 1.7 %table.1 = (bf16[640,1536]{1,0:T(8,128)(2,1)S(1)}, bf16[1536,640]{1,0:T(8,128)(2,1)S(1)}) custom-call(f32[128,768]{1,0:T(8,128)S(1)} %slice.24.bc_ref, f32[128,768]{1,0:T(8,128)S(1)} %slice.25.bs_ref, f32[8,768]{1,0:T(8,128)S(1)} %slice.26.ac_ref, f32[8,768]{1,0:T(8,128)S(1)} %slice.27.as_ref, f32[768,8]{1,0:T(8,128)S(1)} %get-tuple-element.33.cc_ref, ...), custom_call_target="tpu_custom_call" | custom-call | flops 6000000 | bytes 5000000 | tf_op jit(solution)/shard_map/table/pallas_call | solution.py:385
  33.7 1.3 copy-done.7
  35.0 1.3 copy-done.9
  36.3 0.3 fusion.hot_ref
  36.6 8.1 %all-to-all-done.1.x_ref = bf16[48,24,128]{2,1,0:T(8,128)(2,1)S(1)} async-done(((bf16[48,24,128]{2,1,0:T(8,128)(2,1)}), bf16[48,24,128]{2,1,0:T(8,128)(2,1)S(1)}, u32[]{:S(2)}, u32[]{:S(2)}) %all-to-all-start.1) | async-done | bytes 294944 | tf_op jit(solution)/shard_map/all_to_all | solution.py:345
  44.7 1.5 %copy-done.10 = bf16[640,1536]{1,0:T(8,128)(2,1)S(1)} copy-done((bf16[640,1536]{1,0:T(8,128)(2,1)S(1)}, bf16[640,1536]{1,0:T(8,128)(2,1)}, u32[]{:S(2)}) %copy-start.10) | copy-done | bytes 1966104
  46.2 4.3 %surface.1 = bf16[16,128]{1,0:T(8,128)(2,1)S(1)} custom-call(bf16[48,24,128]{2,1,0:T(8,128)(2,1)S(1)} %all-to-all-done.1.x_ref, bf16[640,1536]{1,0:T(8,128)(2,1)S(1)} %copy-done.10, s32[768,1]{1,0:T(8,128)S(1)} %broadcast_in_dim.34.wave_ref, s32[2048]{0:T(1024)S(1)} %get-tuple-element.37.row_ref, bf16[2048,128]{1,0:T(8,128)(2,1)S(1)} %fusion.hot_ref), custom_call_target="tpu_custom_call" | custom-call | flops 1000000000 | bytes 4000000 | tf_op jit(solution)/shard_map/surface/pallas_call | solution.py:416
  50.5 0.0 copy-start.15
  50.5 0.6 copy.34
  51.1 9.1 %all-to-all-start.2 = ((bf16[16,1,128]{2,1,0:T(2,128)(2,1)}), bf16[16,1,128]{2,1,0:T(2,128)(2,1)S(1)}, u32[]{:S(2)}, u32[]{:S(2)}) async-start(bf16[16,1,128]{2,1,0:T(2,128)(2,1)} %copy.34), calls=%async_computation.2 | async-start | bytes 16384 | tf_op jit(solution)/shard_map/all_to_all | solution.py:426
  60.2 1.9 %mix.1 = bf16[48,40,128]{2,1,0:T(8,128)(2,1)} custom-call(bf16[1536,72]{1,0:T(8,128)(2,1)S(1)} %get-tuple-element.17.f0_ref, bf16[1536,72]{1,0:T(8,128)(2,1)S(1)} %get-tuple-element.18.f1_ref, bf16[4,72,256]{2,1,0:T(8,128)(2,1)S(1)} %get-tuple-element.19.w_ref, f32[8,128]{1,0:T(8,128)S(1)} %pad.4.codes_ref), custom_call_target="tpu_custom_call" | custom-call | flops 200000000 | bytes 2000000 | tf_op jit(solution)/shard_map/mix/pallas_call | solution.py:365
  62.1 6.9 %all-to-all-done.2 = bf16[16,1,128]{2,1,0:T(2,128)(2,1)S(1)} async-done(((bf16[16,1,128]{2,1,0:T(2,128)(2,1)}), bf16[16,1,128]{2,1,0:T(2,128)(2,1)S(1)}, u32[]{:S(2)}, u32[]{:S(2)}) %all-to-all-start.2) | async-done | bytes 4128 | tf_op jit(solution)/shard_map/all_to_all | solution.py:426
  69.0 6.2 %all-to-all-start = ((bf16[48,40,128]{2,1,0:T(8,128)(2,1)}), bf16[48,40,128]{2,1,0:T(8,128)(2,1)}, u32[]{:S(2)}, u32[]{:S(2)}) async-start(bf16[48,40,128]{2,1,0:T(8,128)(2,1)} %mix.1), calls=%async_computation | async-start | bytes 983040 | tf_op jit(solution)/shard_map/all_to_all | solution.py:375
  75.2 0.9 fusion.14
  76.1 2.6 %collective-permute-start.1 = (bf16[1044,64]{1,0:T(8,128)(2,1)}, bf16[1044,64]{1,0:T(8,128)(2,1)}, u32[]{:S(2)}, u32[]{:S(2)}) collective-permute-start(bf16[1044,64]{1,0:T(8,128)(2,1)} %get-tuple-element.35), channel_id=1, source_target_pairs={{1,0},{2,1},{3,2},{4,3},{5,4},{6,5},{7,6},{8,7},{9,8},{10,9},{11,1... | collective-permute-start | bytes 400904 | tf_op jit(solution)/shard_map/ppermute | solution.py:350
  78.8 2.8 %collective-permute-start = (bf16[1044,64]{1,0:T(8,128)(2,1)}, bf16[1044,64]{1,0:T(8,128)(2,1)}, u32[]{:S(2)}, u32[]{:S(2)}) collective-permute-start(bf16[1044,64]{1,0:T(8,128)(2,1)} %get-tuple-element.34), channel_id=1, source_target_pairs={{0,1},{1,2},{2,3},{3,4},{4,5},{5,6},{6,7},{7,8},{8,9},{9,10},{10,1... | collective-permute-start | bytes 400904 | tf_op jit(solution)/shard_map/ppermute | solution.py:349
  81.6 0.2 copy.36.coupling_ref
  81.8 1.0 broadcast_in_dim.35.speed_ref
  82.8 0.9 broadcast_in_dim.36.momentum_ref
  83.7 2.1 %collective-permute-done.1 = bf16[1044,64]{1,0:T(8,128)(2,1)} collective-permute-done((bf16[1044,64]{1,0:T(8,128)(2,1)}, bf16[1044,64]{1,0:T(8,128)(2,1)}, u32[]{:S(2)}, u32[]{:S(2)}) %collective-permute-start.1) | collective-permute-done | bytes 133664 | tf_op jit(solution)/shard_map/ppermute | solution.py:350
  85.8 7.0 %collective-permute-done = bf16[1044,64]{1,0:T(8,128)(2,1)} collective-permute-done((bf16[1044,64]{1,0:T(8,128)(2,1)}, bf16[1044,64]{1,0:T(8,128)(2,1)}, u32[]{:S(2)}, u32[]{:S(2)}) %collective-permute-start) | collective-permute-done | bytes 133664 | tf_op jit(solution)/shard_map/ppermute | solution.py:349
  92.8 1.2 pad_maximum_fusion.rims_ref
  94.1 1.0 copy-done.3
  95.1 1.8 %advect.1 = (f32[1044,128]{1,0:T(8,128)S(1)}, f32[1044,128]{1,0:T(8,128)S(1)}) custom-call(bf16[1044,128]{1,0:T(8,128)(2,1)S(1)} %copy-done.1, bf16[1044,128]{1,0:T(8,128)(2,1)S(1)} %pad_maximum_fusion.rims_ref, s32[1,512]{1,0:T(1,128)S(1)} %bitcast.20, s32[1,512]{1,0:T(1,128)S(1)} %bitcast.21, f32[1044,1]{1,0:T(8,128)S(1)} %copy-done.3, ...), custom_call_target="tpu_custom_call" | custom-call | flops 500000000 | bytes 4000000 | tf_op jit(solution)/shard_map/advect/pallas_call | solution.py:395
  96.9 1.0 wave.1
  97.9 1.6 %all-to-all-done.y_ref = bf16[48,40,128]{2,1,0:T(8,128)(2,1)} async-done(((bf16[48,40,128]{2,1,0:T(8,128)(2,1)}), bf16[48,40,128]{2,1,0:T(8,128)(2,1)}, u32[]{:S(2)}, u32[]{:S(2)}) %all-to-all-start) | async-done | bytes 491552 | tf_op jit(solution)/shard_map/all_to_all | solution.py:375
  99.5 11.4 %all-to-all-start.3 = ((f32[48,1,128]{2,1,0:T(1,128)}), f32[48,1,128]{2,1,0:T(1,128)S(1)}, u32[]{:S(2)}, u32[]{:S(2)}) async-start(f32[48,1,128]{2,1,0:T(1,128)} %bitcast.8), calls=%async_computation.3 | async-start | bytes 49152 | tf_op jit(solution)/shard_map/all_to_all | solution.py:437
  110.9 1.5 %copy-done.8 = bf16[1536,640]{1,0:T(8,128)(2,1)S(1)} copy-done((bf16[1536,640]{1,0:T(8,128)(2,1)S(1)}, bf16[1536,640]{1,0:T(8,128)(2,1)}, u32[]{:S(2)}) %copy-start.8) | copy-done | bytes 1966104
  112.5 3.3 %synthesis.1 = (f32[2,72,2560]{2,1,0:T(8,128)S(1)}, s32[48,128]{1,0:T(8,128)S(1)}, bf16[128,6144]{1,0:T(8,128)(2,1)S(1)}) custom-call(bf16[48,40,128]{2,1,0:T(8,128)(2,1)} %all-to-all-done.y_ref, s32[1,768]{1,0:T(1,128)S(1)} %broadcast_in_dim.32.wave_ref, bf16[1536,640]{1,0:T(8,128)(2,1)S(1)} %copy-done.8, s32[1]{0:T(128)} %bitcast.6.base_ref), custom_call_target="tpu_custom_call" | custom-call | flops 1200000000 | bytes 6000000 | tf_op jit(solution)/shard_map/synthesis/pallas_call | solution.py:442
  115.8 5.3 %all-to-all-done.3 = f32[48,1,128]{2,1,0:T(1,128)S(1)} async-done(((f32[48,1,128]{2,1,0:T(1,128)}), f32[48,1,128]{2,1,0:T(1,128)S(1)}, u32[]{:S(2)}, u32[]{:S(2)}) %all-to-all-start.3) | async-done | bytes 24608 | tf_op jit(solution)/shard_map/all_to_all | solution.py:437
  121.1 1.9 %scatter.1 = bf16[16,40,128]{2,1,0:T(8,128)(2,1)} custom-call(f32[48,128]{1,0:T(8,128)S(1)} %bitcast.17, s32[48,128]{1,0:T(8,128)S(1)} %get-tuple-element.28.high_ref, bf16[128,6144]{1,0:T(8,128)(2,1)S(1)} %get-tuple-element.29.hot_ref), custom_call_target="tpu_custom_call" | custom-call | flops 100000000 | bytes 2000000 | tf_op jit(solution)/shard_map/scatter/pallas_call | solution.py:461
  122.9 6.6 %all-to-all-start.4 = ((bf16[16,40,128]{2,1,0:T(8,128)(2,1)}), bf16[16,40,128]{2,1,0:T(8,128)(2,1)S(1)}, u32[]{:S(2)}, u32[]{:S(2)}) async-start(bf16[16,40,128]{2,1,0:T(8,128)(2,1)} %scatter.1), calls=%async_computation.4 | async-start | bytes 327680 | tf_op jit(solution)/shard_map/all_to_all | solution.py:470
  130.2 8.3 %all-to-all-done.4.part_ref = bf16[16,40,128]{2,1,0:T(8,128)(2,1)S(1)} async-done(((bf16[16,40,128]{2,1,0:T(8,128)(2,1)}), bf16[16,40,128]{2,1,0:T(8,128)(2,1)S(1)}, u32[]{:S(2)}, u32[]{:S(2)}) %all-to-all-start.4) | async-done | bytes 163872 | tf_op jit(solution)/shard_map/all_to_all | solution.py:470
  138.5 1.1 final.1
  (35 shorter events, 0.2 us)
Async XLA Ops:
  1.4 1.8 %copy-start = (bf16[16,2,1,72,640]{4,3,2,1,0:T(8,128)(2,1)S(1)}, bf16[16,2,1,72,640]{4,3,2,1,0:T(8,128)(2,1)}, u32[]{:S(2)}) copy-start(bf16[16,2,1,72,640]{4,3,2,1,0:T(8,128)(2,1)} %spec_ref.1) | copy-start | bytes 8847364
  3.3 1.5 %copy-start.4 = (bf16[16,96,640]{2,1,0:T(8,128)(2,1)S(1)}, bf16[16,96,640]{2,1,0:T(8,128)(2,1)}, u32[]{:S(2)}) copy-start(bf16[16,96,640]{2,1,0:T(8,128)(2,1)} %leg_ref.1) | copy-start | bytes 5898244
  4.8 21.8 %copy-start.12 = (s32[768]{0:T(1024)S(1)}, s32[768]{0:T(1024)}, u32[]{:S(2)}) copy-start(s32[768]{0:T(1024)} %param.15) | copy-start | bytes 9220
  8.5 20.2 %copy-start.11 = (f32[72]{0:T(128)S(1)}, f32[72]{0:T(128)}, u32[]{:S(2)}) copy-start(f32[72]{0:T(128)} %mix_ref.1) | copy-start | bytes 868
  8.5 21.6 %copy-start.14 = (s32[2048]{0:T(1024)S(1)}, s32[2048]{0:T(1024)}, u32[]{:S(2)}) copy-start(s32[2048]{0:T(1024)} %param.21) | copy-start | bytes 24580
  8.5 36.2 %all-to-all-start.1 = ((bf16[48,24,128]{2,1,0:T(8,128)(2,1)}), bf16[48,24,128]{2,1,0:T(8,128)(2,1)S(1)}, u32[]{:S(2)}, u32[]{:S(2)}) async-start(bf16[48,24,128]{2,1,0:T(8,128)(2,1)} %get-tuple-element.20), calls=%async_computation.1 | async-start | bytes 589824 | tf_op jit(solution)/shard_map/all_to_all | solution.py:345
  33.7 1.3 copy-start.7
  35.0 1.3 copy-start.9
  44.7 1.5 %copy-start.10 = (bf16[640,1536]{1,0:T(8,128)(2,1)S(1)}, bf16[640,1536]{1,0:T(8,128)(2,1)}, u32[]{:S(2)}) copy-start(bf16[640,1536]{1,0:T(8,128)(2,1)} %copy-done.9) | copy-start | bytes 5898244
  50.5 24.7 %copy-start.1 = (bf16[1044,128]{1,0:T(8,128)(2,1)S(1)}, bf16[1044,128]{1,0:T(8,128)(2,1)}, u32[]{:S(2)}) copy-start(bf16[1044,128]{1,0:T(8,128)(2,1)} %state_ref.1) | copy-start | bytes 801796
  50.5 31.1 %copy-start.13 = (bf16[1044,16]{0,1:T(8,128)(2,1)S(1)}, bf16[1044,16]{0,1:T(8,128)(2,1)}, u32[]{:S(2)}) copy-start(bf16[1044,16]{0,1:T(8,128)(2,1)} %param.16) | copy-start | bytes 100228
  50.5 31.3 %copy-start.15 = (f32[1044]{0:T(1024)S(1)}, f32[1044]{0:T(1024)}, u32[]{:S(2)}) copy-start(f32[1044]{0:T(1024)} %param.18) | copy-start | bytes 12532
  51.1 17.8 %all-to-all-start.2 = ((bf16[16,1,128]{2,1,0:T(2,128)(2,1)}), bf16[16,1,128]{2,1,0:T(2,128)(2,1)S(1)}, u32[]{:S(2)}, u32[]{:S(2)}) async-start(bf16[16,1,128]{2,1,0:T(2,128)(2,1)} %copy.34), calls=%async_computation.2 | async-start | bytes 16384 | tf_op jit(solution)/shard_map/all_to_all | solution.py:426
  62.1 31.9 %copy-start.2 = (bf16[1044,1044]{1,0:T(8,128)(2,1)S(1)}, bf16[1044,1044]{1,0:T(8,128)(2,1)}, u32[]{:S(2)}) copy-start(bf16[1044,1044]{1,0:T(8,128)(2,1)} %inter_ref.1) | copy-start | bytes 6539620
  62.1 31.9 %copy-start.5 = (s32[512]{0:T(512)S(1)}, s32[512]{0:T(512)}, u32[]{:S(2)}) copy-start(s32[512]{0:T(512)} %param.22) | copy-start | bytes 6148
  62.1 31.9 %copy-start.6 = (s32[512]{0:T(512)S(1)}, s32[512]{0:T(512)}, u32[]{:S(2)}) copy-start(s32[512]{0:T(512)} %param.23) | copy-start | bytes 6148
  69.0 30.5 %all-to-all-start = ((bf16[48,40,128]{2,1,0:T(8,128)(2,1)}), bf16[48,40,128]{2,1,0:T(8,128)(2,1)}, u32[]{:S(2)}, u32[]{:S(2)}) async-start(bf16[48,40,128]{2,1,0:T(8,128)(2,1)} %mix.1), calls=%async_computation | async-start | bytes 983040 | tf_op jit(solution)/shard_map/all_to_all | solution.py:375
  76.1 9.7 %collective-permute-start.1 = (bf16[1044,64]{1,0:T(8,128)(2,1)}, bf16[1044,64]{1,0:T(8,128)(2,1)}, u32[]{:S(2)}, u32[]{:S(2)}) collective-permute-start(bf16[1044,64]{1,0:T(8,128)(2,1)} %get-tuple-element.35), channel_id=1, source_target_pairs={{1,0},{2,1},{3,2},{4,3},{5,4},{6,5},{7,6},{8,7},{9,8},{10,9},{11,1... | collective-permute-start | bytes 400904 | tf_op jit(solution)/shard_map/ppermute | solution.py:350
  78.8 14.1 %collective-permute-start = (bf16[1044,64]{1,0:T(8,128)(2,1)}, bf16[1044,64]{1,0:T(8,128)(2,1)}, u32[]{:S(2)}, u32[]{:S(2)}) collective-permute-start(bf16[1044,64]{1,0:T(8,128)(2,1)} %get-tuple-element.34), channel_id=1, source_target_pairs={{0,1},{1,2},{2,3},{3,4},{4,5},{5,6},{6,7},{7,8},{8,9},{9,10},{10,1... | collective-permute-start | bytes 400904 | tf_op jit(solution)/shard_map/ppermute | solution.py:349
  94.0 1.0 copy-start.3
  99.5 21.5 %all-to-all-start.3 = ((f32[48,1,128]{2,1,0:T(1,128)}), f32[48,1,128]{2,1,0:T(1,128)S(1)}, u32[]{:S(2)}, u32[]{:S(2)}) async-start(f32[48,1,128]{2,1,0:T(1,128)} %bitcast.8), calls=%async_computation.3 | async-start | bytes 49152 | tf_op jit(solution)/shard_map/all_to_all | solution.py:437
  110.9 1.5 %copy-start.8 = (bf16[1536,640]{1,0:T(8,128)(2,1)S(1)}, bf16[1536,640]{1,0:T(8,128)(2,1)}, u32[]{:S(2)}) copy-start(bf16[1536,640]{1,0:T(8,128)(2,1)} %copy-done.7) | copy-start | bytes 5898244
  122.9 15.6 %all-to-all-start.4 = ((bf16[16,40,128]{2,1,0:T(8,128)(2,1)}), bf16[16,40,128]{2,1,0:T(8,128)(2,1)S(1)}, u32[]{:S(2)}, u32[]{:S(2)}) async-start(bf16[16,40,128]{2,1,0:T(8,128)(2,1)} %scatter.1), calls=%async_computation.4 | async-start | bytes 327680 | tf_op jit(solution)/shard_map/all_to_all | solution.py:470

commit v2 on v1

v2 whole, which is shorter than its diff:
```python
import functools

import jax
import jax.numpy as jnp
from jax import lax
from jax.experimental import pallas as pl
from jax.experimental.pallas import tpu as pltpu
from jax.sharding import PartitionSpec as P

LON = 2560
RIM = 64
QUARTER = LON // 4
LANES = 128

time_step = 0.25

bf16 = jnp.bfloat16
f32 = jnp.float32
i32 = jnp.int32

NN = (((1,), (0,)), ((), ()))
NT = (((1,), (1,)), ((), ()))

VMEM = pl.BlockSpec(memory_space=pltpu.VMEM)
SMEM = pl.BlockSpec(memory_space=pltpu.SMEM)


def dot(a, b, dims=NN):
    return lax.dot_general(a, b, dims, preferred_element_type=f32)


def after(value, other):
    return lax.optimization_barrier((value, other))[0]


def lane_of(shape):
    return lax.broadcasted_iota(i32, shape, len(shape) - 1)


def params(mib, **more):
    return pltpu.CompilerParams(vmem_limit_bytes=mib << 20, **more)


def cost(flops, nbytes, trans=0):
    return pl.CostEstimate(flops=int(flops), bytes_accessed=int(nbytes), transcendentals=int(trans))


def legendre_kernel(per, slots, wave_ref, leg_ref, spec_ref, f0_ref, f1_ref, x_ref, s0, s1, low):
    step = pl.program_id(0)
    lats, degrees = leg_ref.shape[1:]
    levels = f0_ref.shape[1]

    @pl.when(step == 0)
    def _():
        low[...] = jnp.zeros_like(low)

    column = lane_of((1, degrees))
    lane = lane_of((lats, LANES))
    fill = jnp.zeros((lats, LANES - levels), f32)
    first = lax.axis_index("lat") * slots
    picked = low[0:lats, :]
    for k in range(per):
        slot = step * per + k
        limit = degrees - lax.div(wave_ref[first + slot] * degrees, wave_ref.shape[0])
        weights = jnp.where(column < limit, leg_ref[k].astype(f32), 0.0).astype(bf16)
        for c, store in ((0, s0), (1, s1)):
            sums = dot(weights, spec_ref[k, c, 0], NT)
            store[pl.ds(slot, lats, stride=slots), :] = jnp.concatenate([sums, fill], axis=1)
            lowest = jnp.broadcast_to(sums[:, levels - 1 : levels], (lats, LANES))
            picked = jnp.where(lane == c * slots + slot, lowest, picked)
    low[0:lats, :] = picked

    @pl.when(step == pl.num_programs(0) - 1)
    def _():
        f0_ref[...] = s0[:, 0:levels].astype(bf16)
        f1_ref[...] = s1[:, 0:levels].astype(bf16)
        turned = low[...].T
        tail = turned[24:32, :]
        lane8 = lane_of((8, LANES))
        rows = [
            jnp.where(lane8 < 96, turned[8 * h : 8 * h + 8, :], pltpu.roll(tail, 96 - 32 * h, 1))
            for h in range(3)
        ]
        packed = jnp.concatenate(rows, axis=0).astype(bf16)
        x_ref[...] = jnp.broadcast_to(packed[None], x_ref.shape)


def inverse_kernel(levels, mix_ref, w_ref, col_ref, left, right):
    width = 2 * LANES
    lane = lax.broadcasted_iota(i32, (2, width), 1)
    start = lax.broadcasted_iota(i32, (2, width), 0) * levels
    unit = lane - start
    ratio, part = [], []
    for level in range(levels):
        below = jnp.full((2, width), mix_ref[level], f32)
        rhs = (unit == level).astype(f32)
        if level == 0:
            scale = 1.0 / (1.0 + below)
            part.append(rhs * scale)
        else:
            above = jnp.full((2, width), mix_ref[level - 1], f32)
            scale = 1.0 / (1.0 + below + above - above * ratio[-1])
            part.append((rhs + above * part[-1]) * scale)
        ratio.append(below * scale)
    solved = part[-1]
    for level in range(levels - 1, -1, -1):
        if level < levels - 1:
            solved = part[level] + ratio[level] * solved
        left[2 * level : 2 * level + 2, :] = solved[:, :LANES]
        right[2 * level : 2 * level + 2, :] = solved[:, LANES:]
    for c in range(2):
        block = jnp.concatenate([half[pl.ds(c, levels, stride=2), :] for half in (left, right)], axis=1)
        high = block.astype(bf16)
        w_ref[2 * c] = high
        w_ref[2 * c + 1] = (block - high.astype(f32)).astype(bf16)
        if c == 0:
            col_ref[...] = jnp.broadcast_to(block[:, levels - 1 : levels], col_ref.shape)


def mix_kernel(owners, f0_ref, f1_ref, w_ref, codes_ref, main_ref, tail_ref, rest):
    sums = dot(f0_ref[...], w_ref[0]) + dot(f0_ref[...], w_ref[1])
    sums += dot(f1_ref[...], w_ref[2]) + dot(f1_ref[...], w_ref[3])
    count = sums.shape[0]
    rest[...] = sums[:, LANES:]
    lane = lane_of((count // 4, LANES))
    tail = jnp.broadcast_to(codes_ref[...][None], (owners, 8, LANES)).reshape(count // 4, LANES)
    for g in range(4):
        piece = rest[pl.ds(g, count // 4, stride=4), :]
        if g:
            piece = pltpu.roll(piece, 16 * g, 1)
        tail = jnp.where((lane >= 16 * g) & (lane < 16 * g + 16), piece, tail)
    main_ref[...] = sums[:, :LANES].reshape(owners, count // owners, LANES).astype(bf16)
    tail_ref[...] = tail.reshape(owners, 8, LANES)


def waves(wave_ref):
    slots = wave_ref.shape[1]
    wave = wave_ref[...].astype(f32)

    def angles(count, unit):
        step = lax.broadcasted_iota(i32, (count, slots), 0).astype(f32) * float(unit)
        turn = step * wave
        turn = turn - float(LON) * jnp.floor(turn * (1.0 / LON) + 0.5)
        phase = turn * (2.0 * jnp.pi / LON)
        return jnp.cos(phase), jnp.sin(phase)

    ones = angles(16, 1)
    tens = angles(8, 16)
    parts = [added((tens[0][k : k + 1], tens[1][k : k + 1]), ones) for k in range(8)]
    return [jnp.concatenate([p[c] for p in parts], axis=0) for c in range(2)], angles(8, LANES)


def added(a, b):
    return a[0] * b[0] - a[1] * b[1], a[1] * b[0] + a[0] * b[1]


def long_kernel(wave_ref, long_ref):
    slots = wave_ref.shape[1]
    fine, coarse = waves(wave_ref)
    for a in range(QUARTER // LANES):
        c, s = added((coarse[0][a : a + 1], coarse[1][a : a + 1]), fine)
        rows = slice(a * LANES, (a + 1) * LANES)
        long_ref[rows, 0:slots] = c.astype(bf16)
        long_ref[rows, slots : 2 * slots] = (-s).astype(bf16)


def wide_kernel(wave_ref, wide_ref):
    slots = wave_ref.shape[1]
    fine, coarse = waves(wave_ref)
    for first in range(0, slots, LANES):
        mine = slice(first, first + LANES)
        turned = [x[:, mine].T for x in fine]
        for a in range(QUARTER // LANES):
            start = [jnp.broadcast_to(x[a : a + 1, mine], (LANES, LANES)).T for x in coarse]
            c, s = added(start, turned)
            columns = slice(a * LANES, (a + 1) * LANES)
            wide_ref[mine, columns] = c.astype(bf16)
            wide_ref[slots + first : slots + first + LANES, columns] = (-s).astype(bf16)


def turned_pair(first, second, wave, m):
    if m == 0:
        return first, second
    turns = (wave * m) & 3
    even = (turns & 1) == 0
    sign0 = jnp.where((turns == 0) | (turns == 3), 1.0, -1.0)
    sign1 = jnp.where((turns == 0) | (turns == 1), 1.0, -1.0)
    return jnp.where(even, first, second) * sign0, jnp.where(even, second, first) * sign1


def unpacked(x_ref):
    peers = x_ref.shape[0]
    x = x_ref[...].astype(f32)
    lane = lane_of((peers, 8, LANES))
    tail = jnp.zeros((peers, 8, LANES), f32)
    for h in range(3):
        moved = pltpu.roll(x[:, 8 * h : 8 * h + 8, :].reshape(peers * 8, LANES), 32 + 32 * h, 1)
        tail = jnp.where((lane >= 32 * h) & (lane < 32 * h + 32), moved.reshape(peers, 8, LANES), tail)
    return x[:, 0:16, :], jnp.concatenate([x[:, 16:24, :], tail], axis=1)


def surface_kernel(slots, own_ref, other_ref, long_ref, wave_ref, row_ref, lat_ref, o_ref, surface, picked):
    first = lax.rem(lax.axis_index("lat"), 2) == 0
    own, other = unpacked(own_ref), unpacked(other_ref)
    real, imaginary = [
        jnp.stack([jnp.where(first, a, b), jnp.where(first, b, a)], axis=1).reshape(slots, LANES)
        for a, b in zip(own, other)
    ]
    wave = upright(wave_ref).astype(i32)
    pairs = [turned_pair(real, imaginary, wave, m) for m in range(4)]
    coefficients = jnp.concatenate(
        [jnp.concatenate([p[c].astype(bf16) for p in pairs], axis=1) for c in range(2)], axis=0
    )
    values = dot(long_ref[...], coefficients).astype(bf16).astype(f32)
    for m in range(4):
        surface[m * QUARTER : (m + 1) * QUARTER, :] = values[:, m * LANES : (m + 1) * LANES]

    def fetch(block, carry):
        for u in range(32):
            p = block * 32 + u
            picked[pl.ds(p, 1), :] = surface[pl.ds(row_ref[p], 1), :]
        return carry

    lax.fori_loop(0, picked.shape[0] // 32, fetch, 0)
    row = lax.broadcasted_iota(i32, (LANES, LANES), 0)
    diagonal = row == lane_of((LANES, LANES))
    for k in range(lat_ref.shape[0]):
        mine = slice(k * LANES, (k + 1) * LANES)
        hot = (row == lat_ref[k : k + 1, :]).astype(f32).astype(bf16)
        product = dot(picked[mine, :].astype(bf16), hot)
        o_ref[k : k + 1, :] = jnp.sum(jnp.where(diagonal, product, 0.0), axis=0, keepdims=True)


def upright(row_ref):
    count = row_ref.shape[1]
    parts = []
    for first in range(0, count, LANES):
        size = min(LANES, count - first)
        part = row_ref[:, first : first + size]
        if size < LANES:
            part = jnp.concatenate([part, jnp.zeros((1, LANES - size), f32)], axis=1)
        parts.append(jnp.broadcast_to(part, (LANES, LANES)).T[0:size])
    return jnp.concatenate(parts, axis=0)


def advect_kernel(
    state_ref, low_ref, high_ref, source_ref, target_ref, speed_ref, inter_ref, adv_ref, base_ref, held, sem
):
    fetch = pltpu.make_async_copy(inter_ref, held, sem)
    fetch.start()
    edges = source_ref.shape[1]
    points = state_ref.shape[1]
    source_hot = (lax.broadcasted_iota(i32, (points + 2 * RIM, edges), 0) == source_ref[...]).astype(f32)
    target_hot = (lax.broadcasted_iota(i32, (points, edges), 0) == target_ref[...]).astype(f32)
    source_hot, target_hot = source_hot.astype(bf16), target_hot.astype(bf16)
    routes = dot(source_hot, target_hot, NT)
    counts = dot(jnp.ones((8, edges), bf16), target_hot, NT)[0:1, :]
    none = jnp.zeros((points - RIM, points), f32)
    tables = (
        (low_ref, jnp.concatenate([none, routes[0:RIM]], axis=0)),
        (state_ref, routes[RIM : RIM + points]),
        (high_ref, jnp.concatenate([routes[RIM + points :], none], axis=0)),
    )
    inflow = None
    for values, table in tables:
        high = table.astype(bf16)
        rest = (table - high.astype(f32)).astype(bf16)
        part = dot(values[...], high) + dot(values[...], rest)
        inflow = part if inflow is None else inflow + part
    current = state_ref[...].astype(f32)
    advected = current + upright(speed_ref) * (inflow - counts * current)
    squared = (advected * advected).astype(bf16)
    fetch.wait()
    transfer = dot(held[...], squared)
    adv_ref[...] = time_step * advected
    base_ref[...] = advected + time_step * transfer


def wave_kernel(forcing_ref, coupling_ref, adv_ref, base_ref, momentum_ref, main_ref, tail_ref, next_ref, o_ref):
    growth = jnp.tanh(dot(coupling_ref[...], forcing_ref[...].astype(bf16)))
    wave_new = base_ref[...] + growth * adv_ref[...]
    next_ref[...] = wave_new.astype(bf16)
    stress = jnp.sum(upright(momentum_ref) * growth * wave_new, axis=0, keepdims=True)
    stress = jnp.broadcast_to(stress, (8, LANES))
    high = stress.astype(bf16).astype(f32)
    low = stress - high
    row = lax.broadcasted_iota(i32, (8, LANES), 0)
    lane = lane_of((8, LANES))
    part = jnp.where(row < 6, high, low)
    part = jnp.where((row & 1) == 0, pltpu.roll(part, 64, 1), part)
    joined = jnp.where(((row >= 4) & (lane >= 64))[None], part[None], tail_ref[...])
    o_ref[...] = jnp.concatenate([main_ref[...].astype(f32), joined], axis=1).astype(bf16)


def synthesis_kernel(slots, y_ref, wave_ref, wide_ref, d_ref, rest, lhs):
    levels = d_ref.shape[1]
    peers = y_ref.shape[0]
    y = y_ref[...].astype(f32)
    main = y[:, 0:32, :]
    tail = y[:, 32:40, :].reshape(peers * 8, LANES)
    for g in range(4):
        rest[pl.ds(g, peers * 8, stride=4), :] = pltpu.roll(tail, LANES - 16 * g, 1) if g else tail
    wave = wave_ref[...]
    others = rest[...].reshape(peers, 32, LANES)
    padded = 80
    fill = jnp.zeros((padded - levels, slots), f32)
    for t in range(2):
        a = main[:, 16 * t : 16 * t + 16, :].reshape(slots, LANES).T
        b = others[:, 16 * t : 16 * t + 16, :].reshape(slots, LANES).T
        first = a[0:levels]
        second = jnp.concatenate([a[levels:], b[0 : 2 * levels - LANES]], axis=0)
        for m in range(4):
            p, q = turned_pair(first, second, wave, m)
            rows = slice((t * 4 + m) * padded, (t * 4 + m + 1) * padded)
            lhs[rows, 0:slots] = jnp.concatenate([p, fill], axis=0).astype(bf16)
            lhs[rows, slots : 2 * slots] = jnp.concatenate([q, fill], axis=0).astype(bf16)
    for t in range(2):
        sums = dot(lhs[t * 4 * padded : (t + 1) * 4 * padded, :], wide_ref[...])
        for m in range(4):
            d_ref[t, :, m * QUARTER : (m + 1) * QUARTER] = sums[m * padded : m * padded + levels].astype(bf16)


def scatter_kernel(y_ref, o_ref, tails):
    peers = y_ref.shape[0]
    height = o_ref.shape[1]
    tails[...] = y_ref[...].astype(f32)[:, 32:40, :].reshape(peers * 8, LANES)
    lane = lane_of((peers, LANES))

    def line(k):
        left = pltpu.roll(tails[pl.ds(2 * k, peers, stride=8), :], 64, 1)
        return jnp.where(lane < 64, left, tails[pl.ds(2 * k + 1, peers, stride=8), :])

    v0, v1, high, low = [line(k) for k in range(4)]
    cell = (jnp.abs(v0) - 1.0) + 256.0 * (jnp.abs(v1) - 1.0)
    cell += jnp.where(v0 < 0, 65536.0, 0.0) + jnp.where(v1 < 0, 131072.0, 0.0)
    cell = cell.astype(i32) - lax.axis_index("lat") * (height * LANES)
    upper = cell >> 7
    at = cell & (LANES - 1)
    row = lax.broadcasted_iota(i32, (LANES, LANES), 0)
    sums = None
    for k in range(peers):
        one = slice(k, k + 1)
        inside = row[0:height] == upper[one]
        spread = jnp.concatenate([jnp.where(inside, high[one], 0.0), jnp.where(inside, low[one], 0.0)], axis=0)
        hot = (row == at[one]).astype(f32).astype(bf16)
        both = (spread.astype(bf16), hot)
        sums = [both] if sums is None else sums + [both]
    spread = jnp.concatenate([p[0] for p in sums], axis=1)
    hot = jnp.concatenate([p[1] for p in sums], axis=1)
    total = dot(spread, hot, NT)
    o_ref[...] = jnp.broadcast_to((total[0:height] + total[height:]).astype(bf16)[None], o_ref.shape)


def final_kernel(d_ref, part_ref, col_ref, drag_ref, o_ref):
    stress = jnp.sum(part_ref[...].astype(f32), axis=0)
    push = col_ref[...] * drag_ref[0]
    chunks = LON // LANES
    for t in range(2):
        for k in range(chunks):
            columns = slice(k * LANES, (k + 1) * LANES)
            line = stress[t * chunks + k : t * chunks + k + 1, :]
            o_ref[t, 0, :, columns] = (d_ref[t, :, columns].astype(f32) + push * line).astype(bf16)


def local(
    spectral,
    legendre,
    wave_slot,
    coupling_in,
    interaction,
    bin_speed,
    momentum,
    wave_state,
    cell_index,
    edge_source,
    edge_target,
    surface_drag,
    mixing,
):
    slots, _, _, levels, degrees = spectral.shape
    lats = legendre.shape[1]
    all_slots = wave_slot.shape[0]
    owners = lax.axis_size("lat")
    columns = lax.axis_size("fld")
    bins, points = wave_state.shape
    fld = lax.axis_index("fld")
    shape = jax.ShapeDtypeStruct

    per = 4
    wave_row = wave_slot[None, :]
    f0, f1, packed = pl.pallas_call(
        functools.partial(legendre_kernel, per, slots),
        grid=(slots // per,),
        in_specs=[
            SMEM,
            pl.BlockSpec((per, lats, degrees), lambda i: (i, 0, 0)),
            pl.BlockSpec((per, 2, 1, levels, degrees), lambda i: (i, 0, 0, 0, 0)),
        ],
        out_specs=[
            pl.BlockSpec((lats * slots, levels), lambda i: (0, 0)),
            pl.BlockSpec((lats * slots, levels), lambda i: (0, 0)),
            pl.BlockSpec((owners // 2, 24, LANES), lambda i: (0, 0, 0)),
        ],
        out_shape=[
            shape((lats * slots, levels), bf16),
            shape((lats * slots, levels), bf16),
            shape((owners // 2, 24, LANES), bf16),
        ],
        scratch_shapes=[
            pltpu.VMEM((lats * slots, LANES), f32),
            pltpu.VMEM((lats * slots, LANES), f32),
            pltpu.VMEM((LANES, LANES), f32),
        ],
        compiler_params=params(53),
        cost_estimate=cost(3e8, 5e6),
        name="legendre",
    )(wave_slot, legendre, spectral)
    same_core = [[2 * k + core for k in range(owners // 2)] for core in range(2)]
    own_part = lax.all_to_all(
        packed, "lat", split_axis=0, concat_axis=0, tiled=True, axis_index_groups=same_core
    )
    other_part = lax.ppermute(own_part, "lat", [(k, k ^ 1) for k in range(owners)])
    long = pl.pallas_call(
        long_kernel,
        in_specs=[VMEM],
        out_specs=VMEM,
        out_shape=shape((QUARTER, 2 * all_slots), bf16),
        compiler_params=params(10),
        cost_estimate=cost(6e6, 3e6),
        name="long",
    )(after(wave_row, own_part))

    tiles = owners * columns
    up = [(k, k + 1) for k in range(tiles - 1)]
    low = lax.ppermute(wave_state, ("lat", "fld"), up)
    high = lax.ppermute(wave_state, ("lat", "fld"), [(b, a) for a, b in up])

    lat_row = cell_index // LON
    rows = cell_index - lat_row * LON
    picked = pl.pallas_call(
        functools.partial(surface_kernel, all_slots),
        in_specs=[VMEM, VMEM, VMEM, VMEM, SMEM, VMEM],
        out_specs=VMEM,
        out_shape=shape((columns, points), f32),
        scratch_shapes=[pltpu.VMEM((LON, LANES), f32), pltpu.VMEM((columns * points, LANES), f32)],
        compiler_params=params(14),
        cost_estimate=cost(1e9, 4e6),
        name="surface",
    )(own_part, other_part, long, wave_row.astype(f32), rows, lat_row.reshape(columns, points))
    forcing = lax.all_to_all(picked, "fld", split_axis=0, concat_axis=0, tiled=True)

    mixers, column = pl.pallas_call(
        functools.partial(inverse_kernel, levels),
        in_specs=[SMEM],
        out_specs=[VMEM, VMEM],
        out_shape=[shape((4, levels, 2 * LANES), bf16), shape((levels, LANES), f32)],
        scratch_shapes=[pltpu.VMEM((2 * levels, LANES), f32)] * 2,
        compiler_params=params(4),
        cost_estimate=cost(3e6, 2e5),
        name="inverse",
    )(mixing)
    own_cells = lax.dynamic_slice_in_dim(cell_index, fld * points, points)
    sign0 = 1 - 2 * ((own_cells >> 16) & 1)
    sign1 = 1 - 2 * (own_cells >> 17)
    codes = jnp.stack([((own_cells & 255) + 1) * sign0, (((own_cells >> 8) & 255) + 1) * sign1])
    codes = jnp.pad(codes.astype(f32).reshape(4, 64), ((0, 4), (64, 0)))
    main, tail = pl.pallas_call(
        functools.partial(mix_kernel, owners),
        in_specs=[VMEM] * 4,
        out_specs=[VMEM, VMEM],
        out_shape=[shape((owners, 32, LANES), bf16), shape((owners, 8, LANES), f32)],
        scratch_shapes=[pltpu.VMEM((lats * slots, LANES), f32)],
        compiler_params=params(10),
        cost_estimate=cost(2e8, 2e6),
        name="mix",
    )(f0, f1, mixers, codes)

    adv, base = pl.pallas_call(
        advect_kernel,
        in_specs=[VMEM] * 6 + [pl.BlockSpec(memory_space=pl.ANY)],
        out_specs=[VMEM] * 2,
        out_shape=[shape((bins, points), f32)] * 2,
        scratch_shapes=[pltpu.VMEM((bins, bins), bf16), pltpu.SemaphoreType.DMA],
        compiler_params=params(51),
        cost_estimate=cost(5e8, 4e6),
        name="advect",
    )(
        wave_state,
        low,
        high,
        after(edge_source[None, :], picked),
        edge_target[None, :],
        bin_speed[None, :],
        interaction,
    )

    wave_next, outgoing = pl.pallas_call(
        wave_kernel,
        in_specs=[VMEM] * 7,
        out_specs=[VMEM, VMEM],
        out_shape=[shape((bins, points), bf16), shape((owners, 40, LANES), bf16)],
        compiler_params=params(8),
        cost_estimate=cost(1e7, 2e6, bins * points),
        name="wave",
    )(forcing, coupling_in, adv, base, momentum[None, :], main, tail)
    bulk = lax.all_to_all(outgoing, "lat", split_axis=0, concat_axis=0, tiled=True)

    lat_rows = lats // owners
    partial = pl.pallas_call(
        scatter_kernel,
        in_specs=[VMEM],
        out_specs=VMEM,
        out_shape=shape((columns, lat_rows * LON // LANES, LANES), bf16),
        scratch_shapes=[pltpu.VMEM((owners * 8, LANES), f32)],
        compiler_params=params(8),
        cost_estimate=cost(1e8, 2e6),
        name="scatter",
    )(bulk)
    partials = lax.all_to_all(partial, "fld", split_axis=0, concat_axis=0, tiled=True)

    bulk = after(bulk, partial)
    wide = pl.pallas_call(
        wide_kernel,
        in_specs=[VMEM],
        out_specs=VMEM,
        out_shape=shape((2 * all_slots, QUARTER), bf16),
        compiler_params=params(10),
        cost_estimate=cost(6e6, 3e6),
        name="wide",
    )(after(wave_row, partial))
    mixed_rows = pl.pallas_call(
        functools.partial(synthesis_kernel, all_slots),
        in_specs=[VMEM, VMEM, VMEM],
        out_specs=VMEM,
        out_shape=shape((lat_rows, levels, LON), bf16),
        scratch_shapes=[pltpu.VMEM((owners * 32, LANES), f32), pltpu.VMEM((640, 2 * all_slots), bf16)],
        compiler_params=params(14),
        cost_estimate=cost(1.2e9, 6e6),
        name="synthesis",
    )(bulk, wave_row, wide)

    mixed = pl.pallas_call(
        final_kernel,
        in_specs=[VMEM, VMEM, VMEM, SMEM],
        out_specs=VMEM,
        out_shape=shape((lat_rows, 1, levels, LON), bf16),
        compiler_params=params(6),
        cost_estimate=cost(1e6, 3e6),
        name="final",
    )(mixed_rows, partials, column, surface_drag)
    return (mixed, wave_next)


def solution(mesh):
    in_specs = (
        P("lat", None, "fld", None, None),
        P("lat", None, None),
        P(),
        P(),
        P(),
        P(),
        P(),
        P(None, ("lat", "fld")),
        P("lat"),
        P(("lat", "fld")),
        P(("lat", "fld")),
        P("fld"),
        P(),
    )
    out_specs = (P("lat", "fld", None, None), P(None, ("lat", "fld")))
    return jax.shard_map(local, mesh=mesh, in_specs=in_specs, out_specs=out_specs, check_vma=False)
```

time: 141 us -> 113 us (0.80)
  blocking collectives: 0 us -> 33.4 us
  waiting for transfers between devices: 39.2 us -> 10.8 us
  starting transfers between devices: 56.8 us -> 41.8 us
  local copies, waits for them, and re-layouts: 14.2 us -> 1.11 us
  other arithmetic: 5.66 us -> 0.11 us
  Pallas kernels: 22.1 us -> 23.9 us
    all_to_all x0 -> x1, blocking collectives: none -> 33.4 us  [local(): lax.all_to_all(outgoing, 'lat', split_axis=0, concat_axis=0, tiled=True)]
    all_to_all x3 -> x1, starting transfers between devices: 35.7 us -> 16.8 us  [local(): lax.all_to_all(packed, 'lat', split_axis=0, concat_axis=0, tiled=True, ax...]
    all_to_all x3 -> x1, waiting for transfers between devices: 14.9 us -> 0.01 us  [local(): lax.all_to_all(packed, 'lat', split_axis=0, concat_axis=0, tiled=True, ax...]
    unnamed x34 -> x19, local copies, waits for them, and re-layouts: 10.3 us -> 0.94 us
    ppermute x2 -> x3, waiting for transfers between devices: 9.12 us -> 0.01 us  [the longest x1 0.01 us: local(): low = lax.ppermute(wave_state, ('lat', 'fld'), up)]
    ppermute x2 -> x3, starting transfers between devices: 5.45 us -> 12.6 us  [the longest x1 6.82 us: local(): high = lax.ppermute(wave_state, ('lat', 'fld'), [(b, a) for a, b in up])]
    sin x2 -> x0, other arithmetic: 3.16 us -> none  [angles(): return (jnp.cos(phase), jnp.sin(phase))]
    all_to_all x1, starting transfers between devices: 6.62 us -> 3.52 us  [local(): lax.all_to_all(partial, 'fld', split_axis=0, concat_axis=0, tiled=True)]
  transfers between devices with their start and end apart: 7 -> 6, of which waited for: 7 -> 2; matrix products, arithmetic and copies ran while one was open for 6% -> 0% of each run, Pallas kernels for 8% -> 13%
where the time goes in v2:
time: 113 us
  starting transfers between devices  41.8 us (37%)
  blocking collectives  33.4 us (30%)
  Pallas kernels  23.9 us (21%)
  waiting for transfers between devices  10.8 us (10%)
  between operations  1.53 us (1%)
    all_to_all x1, blocking collectives, local(): lax.all_to_all(outgoing, 'lat', split_axis=0, concat_axis=0, tiled=True)  33.4 us
    all_to_all x1, starting transfers between devices, local(): lax.all_to_all(packed, 'lat', split_axis=0, concat_axis=0, tiled=True, ax...  16.8 us
    all_to_all x1, starting transfers between devices, local(): lax.all_to_all(picked, 'fld', split_axis=0, concat_axis=0, tiled=True)  8.77 us
    ppermute x1, starting transfers between devices, local(): high = lax.ppermute(wave_state, ('lat', 'fld'), [(b, a) for a, b in up])  6.82 us
    all_to_all x1, waiting for transfers between devices, local(): lax.all_to_all(picked, 'fld', split_axis=0, concat_axis=0, tiled=True)  5.44 us
    all_to_all x1, waiting for transfers between devices, local(): lax.all_to_all(partial, 'fld', split_axis=0, concat_axis=0, tiled=True)  5.36 us
    pallas_call x1, Pallas kernels, local(): pl.pallas_call(functools.partial(legendre_kernel, per, slots), grid=(slot...  5.18 us
    pallas_call x1, Pallas kernels, local(): pl.pallas_call(functools.partial(surface_kernel, all_slots), in_specs=[VM...  5.07 us
  transfers between devices with their start and end apart: 6, of which 2 were waited for; matrix products, arithmetic and copies ran while one was open for 0% of the time, Pallas kernels for 13%

profile of v2, /device:TPU:1, one launch (start us, length us, event | category | flops | bytes accessed | tf_op | source)
XLA Modules:
  0.0 112.7 jit_solution(6870828834566677602)
XLA Ops:
  0.6 0.0 copy-start
  0.6 0.0 copy-start.1
  0.7 0.7 copy-done.1
  1.4 0.0 copy-start.6
  1.4 0.0 copy-start.7
  1.4 0.0 copy-start.5
  1.4 0.0 copy-start.8
  1.4 0.0 copy-start.4
  1.4 5.2 %legendre.1 = (bf16[1536,72]{1,0:T(8,128)(2,1)S(1)}, bf16[1536,72]{1,0:T(8,128)(2,1)S(1)}, bf16[24,24,128]{2,1,0:T(8,128)(2,1)}) custom-call(s32[768]{0:T(1024)S(1)} %copy-done.1, bf16[16,96,640]{2,1,0:T(8,128)(2,1)} %leg_ref.1, bf16[16,2,1,72,640]{4,3,2,1,0:T(8,128)(2,1)} %spec_ref.1), custom_call_target="tpu_custom_call" | custom-call | flops 300000000 | bytes 5000000 | tf_op jit(solution)/shard_map/legendre/pallas_call | solution.py:391
  6.6 16.8 %all-to-all-start = ((bf16[24,24,128]{2,1,0:T(8,128)(2,1)}), bf16[24,24,128]{2,1,0:T(8,128)(2,1)S(1)}, u32[]{:S(2)}, u32[]{:S(2)}) async-start(bf16[24,24,128]{2,1,0:T(8,128)(2,1)} %get-tuple-element.17), calls=%async_computation | async-start | bytes 294912 | tf_op jit(solution)/shard_map/all_to_all | solution.py:419
  23.4 0.0 copy-done
  23.4 3.2 %collective-permute-start.1 = (bf16[1044,128]{1,0:T(8,128)(2,1)S(1)}, bf16[1044,128]{1,0:T(8,128)(2,1)S(1)}, u32[]{:S(2)}, u32[]{:S(2)}) collective-permute-start(bf16[1044,128]{1,0:T(8,128)(2,1)S(1)} %copy-done), channel_id=1, source_target_pairs={{0,1},{1,2},{2,3},{3,4},{4,5},{5,6},{6,7},{7,8},{8,9},{9,10},{10,1... | collective-permute-start | bytes 801800 | tf_op jit(solution)/shard_map/ppermute | solution.py:435
  26.7 6.8 %collective-permute-start.2 = (bf16[1044,128]{1,0:T(8,128)(2,1)S(1)}, bf16[1044,128]{1,0:T(8,128)(2,1)S(1)}, u32[]{:S(2)}, u32[]{:S(2)}) collective-permute-start(bf16[1044,128]{1,0:T(8,128)(2,1)S(1)} %copy-done), channel_id=1, source_target_pairs={{1,0},{2,1},{3,2},{4,3},{5,4},{6,5},{7,6},{8,7},{9,8},{10,9},{11,1... | collective-permute-start | bytes 801800 | tf_op jit(solution)/shard_map/ppermute | solution.py:436
  33.5 0.0 copy-done.6
  33.5 0.1 multiply_bitcast_fusion.1
  33.6 0.1 convert_element_type.17
  33.7 0.0 copy-done.7
  33.7 0.0 copy-done.5
  33.7 0.2 copy.17.coupling_ref
  33.9 0.0 copy-done.8
  33.9 0.1 pad.4.codes_ref
  34.0 0.0 copy-done.4
  34.0 1.4 %inverse.1 = (bf16[4,72,256]{2,1,0:T(8,128)(2,1)S(1)}, f32[72,128]{1,0:T(8,128)S(1)}) custom-call(f32[72]{0:T(128)S(1)} %copy-done.4), custom_call_target="tpu_custom_call" | custom-call | flops 3000000 | bytes 200000 | tf_op jit(solution)/shard_map/inverse/pallas_call | solution.py:452
  35.4 1.1 mix.1
  36.5 0.0 all-to-all-done.own_ref
  36.5 2.6 %collective-permute-start = (bf16[24,24,128]{2,1,0:T(8,128)(2,1)S(1)}, bf16[24,24,128]{2,1,0:T(8,128)(2,1)S(1)}, u32[]{:S(2)}, u32[]{:S(2)}) collective-permute-start(bf16[24,24,128]{2,1,0:T(8,128)(2,1)S(1)} %all-to-all-done.own_ref), channel_id=1, source_target_pairs={{0,16},{16,0},{32,48},{48,32},{64,80},{80,64},{96,112},{112,96},{1... | collective-permute-start | bytes 442376 | tf_op jit(solution)/shard_map/ppermute | solution.py:422
  39.2 1.0 long.1.long_ref
  40.2 0.0 copy-start.2
  40.2 0.0 copy-start.3
  40.2 0.0 collective-permute-done.other_ref
  40.2 5.1 %surface.1 = f32[16,128]{1,0:T(8,128)} custom-call(bf16[24,24,128]{2,1,0:T(8,128)(2,1)S(1)} %all-to-all-done.own_ref, bf16[24,24,128]{2,1,0:T(8,128)(2,1)S(1)} %collective-permute-done.other_ref, bf16[640,1536]{1,0:T(8,128)(2,1)S(1)} %long.1.long_ref, f32[1,768]{1,0:T(1,128)S(1)} %convert_element_type.15.wave_ref, s32[2048]{0:T(1024)S(1)} %get-tuple-element.35.row_ref, ...), custom_call_target="tpu_custom_call" | custom-call | flops 1000000000 | bytes 4000000 | tf_op jit(solution)/shard_map/surface/pallas_call | solution.py:440
  45.3 8.8 %all-to-all-start.1 = ((f32[16,1,128]{2,1,0:T(1,128)}), f32[16,1,128]{2,1,0:T(1,128)S(1)}, u32[]{:S(2)}, u32[]{:S(2)}) async-start(f32[16,1,128]{2,1,0:T(1,128)} %bitcast.2), calls=%async_computation.1 | async-start | bytes 16384 | tf_op jit(solution)/shard_map/all_to_all | solution.py:450
  54.0 0.0 collective-permute-done.1.low_ref
  54.1 0.0 collective-permute-done.2.high_ref
  54.1 0.0 copy-done.2
  54.1 0.0 copy-done.3
  54.1 3.2 %advect.1 = (f32[1044,128]{1,0:T(8,128)S(1)}, f32[1044,128]{1,0:T(8,128)S(1)}) custom-call(bf16[1044,128]{1,0:T(8,128)(2,1)S(1)} %copy-done, bf16[1044,128]{1,0:T(8,128)(2,1)S(1)} %collective-permute-done.1.low_ref, bf16[1044,128]{1,0:T(8,128)(2,1)S(1)} %collective-permute-done.2.high_ref, s32[1,512]{1,0:T(1,128)S(1)} %bitcast.13, s32[1,512]{1,0:T(1,128)S(1)} %bitcast.14, ...), custom_call_target="tpu_custom_call" | custom-call | flops 500000000 | bytes 4000000 | tf_op jit(solution)/shard_map/advect/pallas_call | solution.py:478
  57.3 5.4 %all-to-all-done.1 = f32[16,1,128]{2,1,0:T(1,128)S(1)} async-done(((f32[16,1,128]{2,1,0:T(1,128)}), f32[16,1,128]{2,1,0:T(1,128)S(1)}, u32[]{:S(2)}, u32[]{:S(2)}) %all-to-all-start.1) | async-done | bytes 8224 | tf_op jit(solution)/shard_map/all_to_all | solution.py:450
  62.8 1.0 wave.1
  63.8 33.4 %all_to_all.26.y_ref = bf16[48,40,128]{2,1,0:T(8,128)(2,1)S(1)} all-to-all(bf16[48,40,128]{2,1,0:T(8,128)(2,1)S(1)} %get-tuple-element.27), channel_id=1, replica_groups=mesh['lat'=48,'fld'=16] {'lat'}, dimensions={0} | all-to-all | bytes 983040 | tf_op jit(solution)/shard_map/all_to_all | solution.py:506
  97.2 1.4 %scatter.1 = bf16[16,40,128]{2,1,0:T(8,128)(2,1)} custom-call(bf16[48,40,128]{2,1,0:T(8,128)(2,1)S(1)} %all_to_all.26.y_ref), custom_call_target="tpu_custom_call" | custom-call | flops 100000000 | bytes 2000000 | tf_op jit(solution)/shard_map/scatter/pallas_call | solution.py:509
  98.6 3.5 %all-to-all-start.3 = ((bf16[16,40,128]{2,1,0:T(8,128)(2,1)}), bf16[16,40,128]{2,1,0:T(8,128)(2,1)S(1)}, u32[]{:S(2)}, u32[]{:S(2)}) async-start(bf16[16,40,128]{2,1,0:T(8,128)(2,1)} %scatter.1), calls=%async_computation.3 | async-start | bytes 327680 | tf_op jit(solution)/shard_map/all_to_all | solution.py:519
  102.8 1.4 %wide.1.wide_ref = bf16[1536,640]{1,0:T(8,128)(2,1)S(1)} custom-call(s32[1,768]{1,0:T(1,128)S(1)} %broadcast_in_dim.15.wave_ref), custom_call_target="tpu_custom_call" | custom-call | flops 6000000 | bytes 3000000 | tf_op jit(solution)/shard_map/wide/pallas_call | solution.py:522
  104.2 2.0 %synthesis.1.d_ref = bf16[2,72,2560]{2,1,0:T(8,128)(2,1)S(1)} custom-call(bf16[48,40,128]{2,1,0:T(8,128)(2,1)S(1)} %all_to_all.26.y_ref, s32[1,768]{1,0:T(1,128)S(1)} %broadcast_in_dim.15.wave_ref, bf16[1536,640]{1,0:T(8,128)(2,1)S(1)} %wide.1.wide_ref), custom_call_target="tpu_custom_call" | custom-call | flops 1200000000 | bytes 6000000 | tf_op jit(solution)/shard_map/synthesis/pallas_call | solution.py:531
  106.2 5.4 %all-to-all-done.3.part_ref = bf16[16,40,128]{2,1,0:T(8,128)(2,1)S(1)} async-done(((bf16[16,40,128]{2,1,0:T(8,128)(2,1)}), bf16[16,40,128]{2,1,0:T(8,128)(2,1)S(1)}, u32[]{:S(2)}, u32[]{:S(2)}) %all-to-all-start.3) | async-done | bytes 163872 | tf_op jit(solution)/shard_map/all_to_all | solution.py:519
  111.5 1.1 %final.1 = bf16[2,1,72,2560]{3,2,1,0:T(8,128)(2,1)} custom-call(bf16[2,72,2560]{2,1,0:T(8,128)(2,1)S(1)} %synthesis.1.d_ref, bf16[16,40,128]{2,1,0:T(8,128)(2,1)S(1)} %all-to-all-done.3.part_ref, f32[72,128]{1,0:T(8,128)S(1)} %get-tuple-element.30.col_ref, f32[1]{0:T(128)S(6)} %copy.18.drag_ref), custom_call_target="tpu_custom_call" | custom-call | flops 1000000 | bytes 3000000 | tf_op jit(solution)/shard_map/final/pallas_call | solution.py:542
  (7 shorter events, 0.0 us)
Async XLA Ops:
  0.6 22.8 %copy-start = (bf16[1044,128]{1,0:T(8,128)(2,1)S(1)}, bf16[1044,128]{1,0:T(8,128)(2,1)}, u32[]{:S(2)}) copy-start(bf16[1044,128]{1,0:T(8,128)(2,1)} %state_ref.1) | copy-start | bytes 801796
  0.6 0.7 copy-start.1
  1.4 32.1 %copy-start.6 = (s32[2048]{0:T(1024)S(1)}, s32[2048]{0:T(1024)}, u32[]{:S(2)}) copy-start(s32[2048]{0:T(1024)} %param.21) | copy-start | bytes 24580
  1.4 32.3 %copy-start.7 = (f32[1044]{0:T(1024)S(1)}, f32[1044]{0:T(1024)}, u32[]{:S(2)}) copy-start(f32[1044]{0:T(1024)} %param.18) | copy-start | bytes 12532
  1.4 32.3 %copy-start.5 = (bf16[1044,16]{0,1:T(8,128)(2,1)S(1)}, bf16[1044,16]{0,1:T(8,128)(2,1)}, u32[]{:S(2)}) copy-start(bf16[1044,16]{0,1:T(8,128)(2,1)} %param.16) | copy-start | bytes 100228
  1.4 32.5 %copy-start.8 = (f32[1044]{0:T(1024)S(1)}, f32[1044]{0:T(1024)}, u32[]{:S(2)}) copy-start(f32[1044]{0:T(1024)} %param.19) | copy-start | bytes 12532
  1.4 32.6 %copy-start.4 = (f32[72]{0:T(128)S(1)}, f32[72]{0:T(128)}, u32[]{:S(2)}) copy-start(f32[72]{0:T(128)} %mix_ref.1) | copy-start | bytes 868
  6.6 30.0 %all-to-all-start = ((bf16[24,24,128]{2,1,0:T(8,128)(2,1)}), bf16[24,24,128]{2,1,0:T(8,128)(2,1)S(1)}, u32[]{:S(2)}, u32[]{:S(2)}) async-start(bf16[24,24,128]{2,1,0:T(8,128)(2,1)} %get-tuple-element.17), calls=%async_computation | async-start | bytes 294912 | tf_op jit(solution)/shard_map/all_to_all | solution.py:419
  23.4 30.6 %collective-permute-start.1 = (bf16[1044,128]{1,0:T(8,128)(2,1)S(1)}, bf16[1044,128]{1,0:T(8,128)(2,1)S(1)}, u32[]{:S(2)}, u32[]{:S(2)}) collective-permute-start(bf16[1044,128]{1,0:T(8,128)(2,1)S(1)} %copy-done), channel_id=1, source_target_pairs={{0,1},{1,2},{2,3},{3,4},{4,5},{5,6},{6,7},{7,8},{8,9},{9,10},{10,1... | collective-permute-start | bytes 801800 | tf_op jit(solution)/shard_map/ppermute | solution.py:435
  26.7 27.4 %collective-permute-start.2 = (bf16[1044,128]{1,0:T(8,128)(2,1)S(1)}, bf16[1044,128]{1,0:T(8,128)(2,1)S(1)}, u32[]{:S(2)}, u32[]{:S(2)}) collective-permute-start(bf16[1044,128]{1,0:T(8,128)(2,1)S(1)} %copy-done), channel_id=1, source_target_pairs={{1,0},{2,1},{3,2},{4,3},{5,4},{6,5},{7,6},{8,7},{9,8},{10,9},{11,1... | collective-permute-start | bytes 801800 | tf_op jit(solution)/shard_map/ppermute | solution.py:436
  36.5 3.6 %collective-permute-start = (bf16[24,24,128]{2,1,0:T(8,128)(2,1)S(1)}, bf16[24,24,128]{2,1,0:T(8,128)(2,1)S(1)}, u32[]{:S(2)}, u32[]{:S(2)}) collective-permute-start(bf16[24,24,128]{2,1,0:T(8,128)(2,1)S(1)} %all-to-all-done.own_ref), channel_id=1, source_target_pairs={{0,16},{16,0},{32,48},{48,32},{64,80},{80,64},{96,112},{112,96},{1... | collective-permute-start | bytes 442376 | tf_op jit(solution)/shard_map/ppermute | solution.py:422
  40.2 13.9 %copy-start.2 = (s32[512]{0:T(512)S(1)}, s32[512]{0:T(512)}, u32[]{:S(2)}) copy-start(s32[512]{0:T(512)} %param.22) | copy-start | bytes 6148
  40.2 13.9 %copy-start.3 = (s32[512]{0:T(512)S(1)}, s32[512]{0:T(512)}, u32[]{:S(2)}) copy-start(s32[512]{0:T(512)} %param.23) | copy-start | bytes 6148
  45.3 17.5 %all-to-all-start.1 = ((f32[16,1,128]{2,1,0:T(1,128)}), f32[16,1,128]{2,1,0:T(1,128)S(1)}, u32[]{:S(2)}, u32[]{:S(2)}) async-start(f32[16,1,128]{2,1,0:T(1,128)} %bitcast.2), calls=%async_computation.1 | async-start | bytes 16384 | tf_op jit(solution)/shard_map/all_to_all | solution.py:450
  98.6 12.9 %all-to-all-start.3 = ((bf16[16,40,128]{2,1,0:T(8,128)(2,1)}), bf16[16,40,128]{2,1,0:T(8,128)(2,1)S(1)}, u32[]{:S(2)}, u32[]{:S(2)}) async-start(bf16[16,40,128]{2,1,0:T(8,128)(2,1)} %scatter.1), calls=%async_computation.3 | async-start | bytes 327680 | tf_op jit(solution)/shard_map/all_to_all | solution.py:519

commit v3 on v2

--- a/solution.py
+++ b/solution.py
@@ -45,10 +45,11 @@
     return pl.CostEstimate(flops=int(flops), bytes_accessed=int(nbytes), transcendentals=int(trans))
 
 
-def legendre_kernel(per, slots, wave_ref, leg_ref, spec_ref, f0_ref, f1_ref, x_ref, s0, s1, low):
+def legendre_kernel(per, slots, wave_ref, leg_ref, spec_ref, f_ref, x_ref, s0, s1, low):
     step = pl.program_id(0)
     lats, degrees = leg_ref.shape[1:]
-    levels = f0_ref.shape[1]
+    both = f_ref.shape[1]
+    levels = both // 2
 
     @pl.when(step == 0)
     def _():
@@ -56,24 +57,24 @@
 
     column = lane_of((1, degrees))
     lane = lane_of((lats, LANES))
-    fill = jnp.zeros((lats, LANES - levels), f32)
+    fill = jnp.zeros((lats, 2 * LANES - both), f32)
     first = lax.axis_index("lat") * slots
     picked = low[0:lats, :]
     for k in range(per):
         slot = step * per + k
         limit = degrees - lax.div(wave_ref[first + slot] * degrees, wave_ref.shape[0])
         weights = jnp.where(column < limit, leg_ref[k].astype(f32), 0.0).astype(bf16)
-        for c, store in ((0, s0), (1, s1)):
-            sums = dot(weights, spec_ref[k, c, 0], NT)
-            store[pl.ds(slot, lats, stride=slots), :] = jnp.concatenate([sums, fill], axis=1)
-            lowest = jnp.broadcast_to(sums[:, levels - 1 : levels], (lats, LANES))
+        sums = dot(weights, spec_ref[k], NT)
+        s0[pl.ds(slot, lats, stride=slots), :] = sums[:, 0:LANES]
+        s1[pl.ds(slot, lats, stride=slots), :] = jnp.concatenate([sums[:, LANES:], fill], axis=1)
+        for c in range(2):
+            lowest = jnp.broadcast_to(sums[:, (c + 1) * levels - 1 : (c + 1) * levels], (lats, LANES))
             picked = jnp.where(lane == c * slots + slot, lowest, picked)
     low[0:lats, :] = picked
 
     @pl.when(step == pl.num_programs(0) - 1)
     def _():
-        f0_ref[...] = s0[:, 0:levels].astype(bf16)
-        f1_ref[...] = s1[:, 0:levels].astype(bf16)
+        f_ref[...] = jnp.concatenate([s0[...], s1[:, 0 : both - LANES]], axis=1).astype(bf16)
         turned = low[...].T
         tail = turned[24:32, :]
         lane8 = lane_of((8, LANES))
@@ -85,7 +86,7 @@
         x_ref[...] = jnp.broadcast_to(packed[None], x_ref.shape)
 
 
-def inverse_kernel(levels, mix_ref, w_ref, col_ref, left, right):
+def inverse(levels, mix_ref, col_ref, left, right):
     width = 2 * LANES
     lane = lax.broadcasted_iota(i32, (2, width), 1)
     start = lax.broadcasted_iota(i32, (2, width), 0) * levels
@@ -108,18 +109,17 @@
             solved = part[level] + ratio[level] * solved
         left[2 * level : 2 * level + 2, :] = solved[:, :LANES]
         right[2 * level : 2 * level + 2, :] = solved[:, LANES:]
-    for c in range(2):
-        block = jnp.concatenate([half[pl.ds(c, levels, stride=2), :] for half in (left, right)], axis=1)
-        high = block.astype(bf16)
-        w_ref[2 * c] = high
-        w_ref[2 * c + 1] = (block - high.astype(f32)).astype(bf16)
-        if c == 0:
-            col_ref[...] = jnp.broadcast_to(block[:, levels - 1 : levels], col_ref.shape)
-
-
-def mix_kernel(owners, f0_ref, f1_ref, w_ref, codes_ref, main_ref, tail_ref, rest):
-    sums = dot(f0_ref[...], w_ref[0]) + dot(f0_ref[...], w_ref[1])
-    sums += dot(f1_ref[...], w_ref[2]) + dot(f1_ref[...], w_ref[3])
+    blocks = [
+        jnp.concatenate([half[pl.ds(c, levels, stride=2), :] for half in (left, right)], axis=1) for c in range(2)
+    ]
+    col_ref[...] = jnp.broadcast_to(blocks[0][:, levels - 1 : levels], col_ref.shape)
+    return jnp.concatenate(blocks, axis=0)
+
+
+def mix_kernel(owners, mix_ref, f_ref, codes_ref, main_ref, tail_ref, col_ref, rest, left, right):
+    mixer = inverse(f_ref.shape[1] // 2, mix_ref, col_ref, left, right)
+    high = mixer.astype(bf16)
+    sums = dot(f_ref[...], high) + dot(f_ref[...], (mixer - high.astype(f32)).astype(bf16))
     count = sums.shape[0]
     rest[...] = sums[:, LANES:]
     lane = lane_of((count // 4, LANES))
@@ -178,14 +178,17 @@
             wide_ref[slots + first : slots + first + LANES, columns] = (-s).astype(bf16)
 
 
-def turned_pair(first, second, wave, m):
-    if m == 0:
-        return first, second
-    turns = (wave * m) & 3
-    even = (turns & 1) == 0
-    sign0 = jnp.where((turns == 0) | (turns == 3), 1.0, -1.0)
-    sign1 = jnp.where((turns == 0) | (turns == 1), 1.0, -1.0)
-    return jnp.where(even, first, second) * sign0, jnp.where(even, second, first) * sign1
+def quarters(wave):
+    turns = wave & 3
+    cos = jnp.where(turns == 0, 1.0, jnp.where(turns == 2, -1.0, 0.0))
+    sin = jnp.where(turns == 1, 1.0, jnp.where(turns == 3, -1.0, 0.0))
+    return cos, sin, jnp.where((turns & 1) == 0, 1.0, -1.0)
+
+
+def turned(first, second, quarter):
+    cos, sin, half = quarter
+    fc, fs, sc, ss = first * cos, first * sin, second * cos, second * sin
+    return [(first, second), (fc - ss, fs + sc), (first * half, second * half), (fc + ss, sc - fs)]
 
 
 def unpacked(x_ref):
@@ -206,8 +209,7 @@
         jnp.stack([jnp.where(first, a, b), jnp.where(first, b, a)], axis=1).reshape(slots, LANES)
         for a, b in zip(own, other)
     ]
-    wave = upright(wave_ref).astype(i32)
-    pairs = [turned_pair(real, imaginary, wave, m) for m in range(4)]
+    pairs = turned(real, imaginary, [upright(x) for x in quarters(wave_ref[...])])
     coefficients = jnp.concatenate(
         [jnp.concatenate([p[c].astype(bf16) for p in pairs], axis=1) for c in range(2)], axis=0
     )
@@ -216,12 +218,13 @@
         surface[m * QUARTER : (m + 1) * QUARTER, :] = values[:, m * LANES : (m + 1) * LANES]
 
     def fetch(block, carry):
-        for u in range(32):
-            p = block * 32 + u
-            picked[pl.ds(p, 1), :] = surface[pl.ds(row_ref[p], 1), :]
+        start = pl.multiple_of(block * LANES, LANES)
+        window = picked.at[pl.ds(start, LANES), :]
+        for u in range(LANES):
+            window[u : u + 1, :] = surface[pl.ds(row_ref[start + u], 1), :]
         return carry
 
-    lax.fori_loop(0, picked.shape[0] // 32, fetch, 0)
+    lax.fori_loop(0, picked.shape[0] // LANES, fetch, 0)
     row = lax.broadcasted_iota(i32, (LANES, LANES), 0)
     diagonal = row == lane_of((LANES, LANES))
     for k in range(lat_ref.shape[0]):
@@ -232,11 +235,12 @@
 
 
 def upright(row_ref):
-    count = row_ref.shape[1]
+    row = row_ref[...]
+    count = row.shape[1]
     parts = []
     for first in range(0, count, LANES):
         size = min(LANES, count - first)
-        part = row_ref[:, first : first + size]
+        part = row[:, first : first + size]
         if size < LANES:
             part = jnp.concatenate([part, jnp.zeros((1, LANES - size), f32)], axis=1)
         parts.append(jnp.broadcast_to(part, (LANES, LANES)).T[0:size])
@@ -300,7 +304,7 @@
     tail = y[:, 32:40, :].reshape(peers * 8, LANES)
     for g in range(4):
         rest[pl.ds(g, peers * 8, stride=4), :] = pltpu.roll(tail, LANES - 16 * g, 1) if g else tail
-    wave = wave_ref[...]
+    quarter = quarters(wave_ref[...])
     others = rest[...].reshape(peers, 32, LANES)
     padded = 80
     fill = jnp.zeros((padded - levels, slots), f32)
@@ -309,8 +313,7 @@
         b = others[:, 16 * t : 16 * t + 16, :].reshape(slots, LANES).T
         first = a[0:levels]
         second = jnp.concatenate([a[levels:], b[0 : 2 * levels - LANES]], axis=0)
-        for m in range(4):
-            p, q = turned_pair(first, second, wave, m)
+        for m, (p, q) in enumerate(turned(first, second, quarter)):
             rows = slice((t * 4 + m) * padded, (t * 4 + m + 1) * padded)
             lhs[rows, 0:slots] = jnp.concatenate([p, fill], axis=0).astype(bf16)
             lhs[rows, slots : 2 * slots] = jnp.concatenate([q, fill], axis=0).astype(bf16)
@@ -388,24 +391,19 @@
 
     per = 4
     wave_row = wave_slot[None, :]
-    f0, f1, packed = pl.pallas_call(
+    sums, packed = pl.pallas_call(
         functools.partial(legendre_kernel, per, slots),
         grid=(slots // per,),
         in_specs=[
             SMEM,
             pl.BlockSpec((per, lats, degrees), lambda i: (i, 0, 0)),
-            pl.BlockSpec((per, 2, 1, levels, degrees), lambda i: (i, 0, 0, 0, 0)),
+            pl.BlockSpec((per, 2 * levels, degrees), lambda i: (i, 0, 0)),
         ],
         out_specs=[
-            pl.BlockSpec((lats * slots, levels), lambda i: (0, 0)),
-            pl.BlockSpec((lats * slots, levels), lambda i: (0, 0)),
+            pl.BlockSpec((lats * slots, 2 * levels), lambda i: (0, 0)),
             pl.BlockSpec((owners // 2, 24, LANES), lambda i: (0, 0, 0)),
         ],
-        out_shape=[
-            shape((lats * slots, levels), bf16),
-            shape((lats * slots, levels), bf16),
-            shape((owners // 2, 24, LANES), bf16),
-        ],
+        out_shape=[shape((lats * slots, 2 * levels), bf16), shape((owners // 2, 24, LANES), bf16)],
         scratch_shapes=[
             pltpu.VMEM((lats * slots, LANES), f32),
             pltpu.VMEM((lats * slots, LANES), f32),
@@ -414,7 +412,7 @@
         compiler_params=params(53),
         cost_estimate=cost(3e8, 5e6),
         name="legendre",
-    )(wave_slot, legendre, spectral)
+    )(wave_slot, legendre, spectral.reshape(slots, 2 * levels, degrees))
     same_core = [[2 * k + core for k in range(owners // 2)] for core in range(2)]
     own_part = lax.all_to_all(
         packed, "lat", split_axis=0, concat_axis=0, tiled=True, axis_index_groups=same_core
@@ -446,34 +444,28 @@
         compiler_params=params(14),
         cost_estimate=cost(1e9, 4e6),
         name="surface",
-    )(own_part, other_part, long, wave_row.astype(f32), rows, lat_row.reshape(columns, points))
+    )(own_part, other_part, long, wave_row, rows, lat_row.reshape(columns, points))
     forcing = lax.all_to_all(picked, "fld", split_axis=0, concat_axis=0, tiled=True)
 
-    mixers, column = pl.pallas_call(
-        functools.partial(inverse_kernel, levels),
-        in_specs=[SMEM],
-        out_specs=[VMEM, VMEM],
-        out_shape=[shape((4, levels, 2 * LANES), bf16), shape((levels, LANES), f32)],
-        scratch_shapes=[pltpu.VMEM((2 * levels, LANES), f32)] * 2,
-        compiler_params=params(4),
-        cost_estimate=cost(3e6, 2e5),
-        name="inverse",
-    )(mixing)
     own_cells = lax.dynamic_slice_in_dim(cell_index, fld * points, points)
     sign0 = 1 - 2 * ((own_cells >> 16) & 1)
     sign1 = 1 - 2 * (own_cells >> 17)
     codes = jnp.stack([((own_cells & 255) + 1) * sign0, (((own_cells >> 8) & 255) + 1) * sign1])
     codes = jnp.pad(codes.astype(f32).reshape(4, 64), ((0, 4), (64, 0)))
-    main, tail = pl.pallas_call(
+    main, tail, column = pl.pallas_call(
         functools.partial(mix_kernel, owners),
-        in_specs=[VMEM] * 4,
-        out_specs=[VMEM, VMEM],
-        out_shape=[shape((owners, 32, LANES), bf16), shape((owners, 8, LANES), f32)],
-        scratch_shapes=[pltpu.VMEM((lats * slots, LANES), f32)],
+        in_specs=[SMEM, VMEM, VMEM],
+        out_specs=[VMEM] * 3,
+        out_shape=[
+            shape((owners, 32, LANES), bf16),
+            shape((owners, 8, LANES), f32),
+            shape((levels, LANES), f32),
+        ],
+        scratch_shapes=[pltpu.VMEM((lats * slots, LANES), f32)] + [pltpu.VMEM((2 * levels, LANES), f32)] * 2,
         compiler_params=params(10),
         cost_estimate=cost(2e8, 2e6),
         name="mix",
-    )(f0, f1, mixers, codes)
+    )(mixing, sums, codes)
 
     adv, base = pl.pallas_call(
         advect_kernel,

time: 113 us -> 113 us (level)
    pallas_call x2 -> x1, Pallas kernels: 2.53 us -> 2.05 us  [local(): pl.pallas_call(functools.partial(mix_kernel, owners), in_specs=[SMEM, VME...]
where the time goes in v3:
time: 113 us; the launch traced here: 112 us
  starting transfers between devices  42.2 us (37%)
  blocking collectives  32.9 us (29%)
  Pallas kernels  23.1 us (20%)
  waiting for transfers between devices  10.8 us (10%)
  between operations  1.54 us (1%)
    all_to_all x1, blocking collectives, local(): lax.all_to_all(outgoing, 'lat', split_axis=0, concat_axis=0, tiled=True)  32.9 us
    all_to_all x1, starting transfers between devices, local(): lax.all_to_all(packed, 'lat', split_axis=0, concat_axis=0, tiled=True, ax...  16.9 us
    all_to_all x1, starting transfers between devices, local(): lax.all_to_all(picked, 'fld', split_axis=0, concat_axis=0, tiled=True)  8.78 us
    ppermute x1, starting transfers between devices, local(): high = lax.ppermute(wave_state, ('lat', 'fld'), [(b, a) for a, b in up])  6.82 us
    all_to_all x1, waiting for transfers between devices, local(): lax.all_to_all(picked, 'fld', split_axis=0, concat_axis=0, tiled=True)  5.44 us
    all_to_all x1, waiting for transfers between devices, local(): lax.all_to_all(partial, 'fld', split_axis=0, concat_axis=0, tiled=True)  5.34 us
    pallas_call x1, Pallas kernels, local(): pl.pallas_call(functools.partial(legendre_kernel, per, slots), grid=(slot...  5.24 us
    pallas_call x1, Pallas kernels, local(): pl.pallas_call(functools.partial(surface_kernel, all_slots), in_specs=[VM...  4.66 us
  transfers between devices with their start and end apart: 6, of which 2 were waited for; matrix products, arithmetic and copies ran while one was open for 0% of the time, Pallas kernels for 13%

profile of v3, /device:TPU:1, one launch (start us, length us, event | category | flops | bytes accessed | tf_op | source)
XLA Modules:
  0.0 111.8 jit_solution(6461399889466958127)
XLA Ops:
  0.6 0.0 copy-start.1
  0.6 0.7 copy-done.1
  1.3 0.0 copy-start
  1.3 0.0 copy-start.2
  1.3 0.0 copy-start.8
  1.3 0.0 copy-start.7
  1.3 0.0 copy-start.6
  1.3 0.0 copy-start.9
  1.4 0.0 copy-start.5
  1.4 5.2 %legendre.1 = (bf16[1536,144]{1,0:T(8,128)(2,1)S(1)}, bf16[24,24,128]{2,1,0:T(8,128)(2,1)}) custom-call(s32[768]{0:T(1024)S(1)} %copy-done.1, bf16[16,96,640]{2,1,0:T(8,128)(2,1)} %leg_ref.1, bf16[16,144,640]{2,1,0:T(8,128)(2,1)} %bitcast.16), custom_call_target="tpu_custom_call" | custom-call | flops 300000000 | bytes 5000000 | tf_op jit(solution)/shard_map/legendre/pallas_call | solution.py:394
  6.6 16.9 %all-to-all-start = ((bf16[24,24,128]{2,1,0:T(8,128)(2,1)}), bf16[24,24,128]{2,1,0:T(8,128)(2,1)S(1)}, u32[]{:S(2)}, u32[]{:S(2)}) async-start(bf16[24,24,128]{2,1,0:T(8,128)(2,1)} %get-tuple-element.15), calls=%async_computation | async-start | bytes 294912 | tf_op jit(solution)/shard_map/all_to_all | solution.py:417
  23.5 0.0 copy-done
  23.5 3.2 %collective-permute-start.1 = (bf16[1044,128]{1,0:T(8,128)(2,1)S(1)}, bf16[1044,128]{1,0:T(8,128)(2,1)S(1)}, u32[]{:S(2)}, u32[]{:S(2)}) collective-permute-start(bf16[1044,128]{1,0:T(8,128)(2,1)S(1)} %copy-done), channel_id=1, source_target_pairs={{0,1},{1,2},{2,3},{3,4},{4,5},{5,6},{6,7},{7,8},{8,9},{9,10},{10,1... | collective-permute-start | bytes 801800 | tf_op jit(solution)/shard_map/ppermute | solution.py:433
  26.7 6.8 %collective-permute-start.2 = (bf16[1044,128]{1,0:T(8,128)(2,1)S(1)}, bf16[1044,128]{1,0:T(8,128)(2,1)S(1)}, u32[]{:S(2)}, u32[]{:S(2)}) collective-permute-start(bf16[1044,128]{1,0:T(8,128)(2,1)S(1)} %copy-done), channel_id=1, source_target_pairs={{1,0},{2,1},{3,2},{4,3},{5,4},{6,5},{7,6},{8,7},{9,8},{10,9},{11,1... | collective-permute-start | bytes 801800 | tf_op jit(solution)/shard_map/ppermute | solution.py:434
  33.5 0.0 copy-done.2
  33.5 0.0 copy-done.8
  33.6 0.0 copy-done.7
  33.6 0.1 multiply_bitcast_fusion.1
  33.7 0.1 convert_element_type.10
  33.8 0.0 copy-done.6
  33.8 0.2 copy.17.coupling_ref
  33.9 0.0 copy-done.9
  34.0 0.1 pad.4.codes_ref
  34.0 0.0 copy-done.5
  34.0 2.0 %mix.1 = (bf16[48,32,128]{2,1,0:T(8,128)(2,1)S(1)}, f32[48,8,128]{2,1,0:T(8,128)S(1)}, f32[72,128]{1,0:T(8,128)S(1)}) custom-call(f32[72]{0:T(128)S(1)} %copy-done.5, bf16[1536,144]{1,0:T(8,128)(2,1)S(1)} %get-tuple-element.20.f_ref, f32[8,128]{1,0:T(8,128)S(1)} %pad.4.codes_ref), custom_call_target="tpu_custom_call" | custom-call | flops 200000000 | bytes 2000000 | tf_op jit(solution)/shard_map/mix/pallas_call | solution.py:455
  36.1 0.0 all-to-all-done.own_ref
  36.1 3.1 %collective-permute-start = (bf16[24,24,128]{2,1,0:T(8,128)(2,1)S(1)}, bf16[24,24,128]{2,1,0:T(8,128)(2,1)S(1)}, u32[]{:S(2)}, u32[]{:S(2)}) collective-permute-start(bf16[24,24,128]{2,1,0:T(8,128)(2,1)S(1)} %all-to-all-done.own_ref), channel_id=1, source_target_pairs={{0,16},{16,0},{32,48},{48,32},{64,80},{80,64},{96,112},{112,96},{1... | collective-permute-start | bytes 442376 | tf_op jit(solution)/shard_map/ppermute | solution.py:420
  39.2 1.0 long.1.long_ref
  40.2 0.0 copy-start.3
  40.2 0.0 copy-start.4
  40.2 0.0 collective-permute-done.other_ref
  40.2 4.7 %surface.1 = f32[16,128]{1,0:T(8,128)} custom-call(bf16[24,24,128]{2,1,0:T(8,128)(2,1)S(1)} %all-to-all-done.own_ref, bf16[24,24,128]{2,1,0:T(8,128)(2,1)S(1)} %collective-permute-done.other_ref, bf16[640,1536]{1,0:T(8,128)(2,1)S(1)} %long.1.long_ref, s32[1,768]{1,0:T(1,128)S(1)} %broadcast_in_dim.15.wave_ref, s32[2048]{0:T(1024)S(1)} %get-tuple-element.31.row_ref, ...), custom_call_target="tpu_custom_call" | custom-call | flops 1000000000 | bytes 4000000 | tf_op jit(solution)/shard_map/surface/pallas_call | solution.py:438
  44.9 8.8 %all-to-all-start.1 = ((f32[16,1,128]{2,1,0:T(1,128)}), f32[16,1,128]{2,1,0:T(1,128)S(1)}, u32[]{:S(2)}, u32[]{:S(2)}) async-start(f32[16,1,128]{2,1,0:T(1,128)} %bitcast.3), calls=%async_computation.1 | async-start | bytes 16384 | tf_op jit(solution)/shard_map/all_to_all | solution.py:448
  53.7 0.0 collective-permute-done.1.low_ref
  53.7 0.0 collective-permute-done.2.high_ref
  53.7 0.0 copy-done.3
  53.7 0.0 copy-done.4
  53.7 3.2 %advect.1 = (f32[1044,128]{1,0:T(8,128)S(1)}, f32[1044,128]{1,0:T(8,128)S(1)}) custom-call(bf16[1044,128]{1,0:T(8,128)(2,1)S(1)} %copy-done, bf16[1044,128]{1,0:T(8,128)(2,1)S(1)} %collective-permute-done.1.low_ref, bf16[1044,128]{1,0:T(8,128)(2,1)S(1)} %collective-permute-done.2.high_ref, s32[1,512]{1,0:T(1,128)S(1)} %bitcast.14, s32[1,512]{1,0:T(1,128)S(1)} %bitcast.15, ...), custom_call_target="tpu_custom_call" | custom-call | flops 500000000 | bytes 4000000 | tf_op jit(solution)/shard_map/advect/pallas_call | solution.py:470
  57.0 5.4 %all-to-all-done.1 = f32[16,1,128]{2,1,0:T(1,128)S(1)} async-done(((f32[16,1,128]{2,1,0:T(1,128)}), f32[16,1,128]{2,1,0:T(1,128)S(1)}, u32[]{:S(2)}, u32[]{:S(2)}) %all-to-all-start.1) | async-done | bytes 8224 | tf_op jit(solution)/shard_map/all_to_all | solution.py:448
  62.4 1.0 wave.1
  63.4 32.9 %all_to_all.26.y_ref = bf16[48,40,128]{2,1,0:T(8,128)(2,1)S(1)} all-to-all(bf16[48,40,128]{2,1,0:T(8,128)(2,1)S(1)} %get-tuple-element.23), channel_id=1, replica_groups=mesh['lat'=48,'fld'=16] {'lat'}, dimensions={0} | all-to-all | bytes 983040 | tf_op jit(solution)/shard_map/all_to_all | solution.py:498
  96.3 1.4 %scatter.1 = bf16[16,40,128]{2,1,0:T(8,128)(2,1)} custom-call(bf16[48,40,128]{2,1,0:T(8,128)(2,1)S(1)} %all_to_all.26.y_ref), custom_call_target="tpu_custom_call" | custom-call | flops 100000000 | bytes 2000000 | tf_op jit(solution)/shard_map/scatter/pallas_call | solution.py:501
  97.7 3.5 %all-to-all-start.3 = ((bf16[16,40,128]{2,1,0:T(8,128)(2,1)}), bf16[16,40,128]{2,1,0:T(8,128)(2,1)S(1)}, u32[]{:S(2)}, u32[]{:S(2)}) async-start(bf16[16,40,128]{2,1,0:T(8,128)(2,1)} %scatter.1), calls=%async_computation.3 | async-start | bytes 327680 | tf_op jit(solution)/shard_map/all_to_all | solution.py:511
  101.9 1.4 %wide.1.wide_ref = bf16[1536,640]{1,0:T(8,128)(2,1)S(1)} custom-call(s32[1,768]{1,0:T(1,128)S(1)} %broadcast_in_dim.15.wave_ref), custom_call_target="tpu_custom_call" | custom-call | flops 6000000 | bytes 3000000 | tf_op jit(solution)/shard_map/wide/pallas_call | solution.py:514
  103.3 2.0 %synthesis.1.d_ref = bf16[2,72,2560]{2,1,0:T(8,128)(2,1)S(1)} custom-call(bf16[48,40,128]{2,1,0:T(8,128)(2,1)S(1)} %all_to_all.26.y_ref, s32[1,768]{1,0:T(1,128)S(1)} %broadcast_in_dim.15.wave_ref, bf16[1536,640]{1,0:T(8,128)(2,1)S(1)} %wide.1.wide_ref), custom_call_target="tpu_custom_call" | custom-call | flops 1200000000 | bytes 6000000 | tf_op jit(solution)/shard_map/synthesis/pallas_call | solution.py:523
  105.3 5.3 %all-to-all-done.3.part_ref = bf16[16,40,128]{2,1,0:T(8,128)(2,1)S(1)} async-done(((bf16[16,40,128]{2,1,0:T(8,128)(2,1)}), bf16[16,40,128]{2,1,0:T(8,128)(2,1)S(1)}, u32[]{:S(2)}, u32[]{:S(2)}) %all-to-all-start.3) | async-done | bytes 163872 | tf_op jit(solution)/shard_map/all_to_all | solution.py:511
  110.7 1.1 %final.1 = bf16[2,1,72,2560]{3,2,1,0:T(8,128)(2,1)} custom-call(bf16[2,72,2560]{2,1,0:T(8,128)(2,1)S(1)} %synthesis.1.d_ref, bf16[16,40,128]{2,1,0:T(8,128)(2,1)S(1)} %all-to-all-done.3.part_ref, f32[72,128]{1,0:T(8,128)S(1)} %get-tuple-element.26.col_ref, f32[1]{0:T(128)S(6)} %copy.18.drag_ref), custom_call_target="tpu_custom_call" | custom-call | flops 1000000 | bytes 3000000 | tf_op jit(solution)/shard_map/final/pallas_call | solution.py:534
  (5 shorter events, 0.0 us)
Async XLA Ops:
  0.6 0.7 copy-start.1
  1.3 22.1 %copy-start = (bf16[1044,128]{1,0:T(8,128)(2,1)S(1)}, bf16[1044,128]{1,0:T(8,128)(2,1)}, u32[]{:S(2)}) copy-start(bf16[1044,128]{1,0:T(8,128)(2,1)} %state_ref.1) | copy-start | bytes 801796
  1.3 32.2 %copy-start.2 = (s32[768]{0:T(1024)S(1)}, s32[768]{0:T(1024)}, u32[]{:S(2)}) copy-start(s32[768]{0:T(1024)} %wave_ref.1) | copy-start | bytes 9220
  1.3 32.2 %copy-start.8 = (f32[1044]{0:T(1024)S(1)}, f32[1044]{0:T(1024)}, u32[]{:S(2)}) copy-start(f32[1044]{0:T(1024)} %param.18) | copy-start | bytes 12532
  1.3 32.2 %copy-start.7 = (s32[2048]{0:T(1024)S(1)}, s32[2048]{0:T(1024)}, u32[]{:S(2)}) copy-start(s32[2048]{0:T(1024)} %param.21) | copy-start | bytes 24580
  1.3 32.4 %copy-start.6 = (bf16[1044,16]{0,1:T(8,128)(2,1)S(1)}, bf16[1044,16]{0,1:T(8,128)(2,1)}, u32[]{:S(2)}) copy-start(bf16[1044,16]{0,1:T(8,128)(2,1)} %param.16) | copy-start | bytes 100228
  1.3 32.6 %copy-start.9 = (f32[1044]{0:T(1024)S(1)}, f32[1044]{0:T(1024)}, u32[]{:S(2)}) copy-start(f32[1044]{0:T(1024)} %param.19) | copy-start | bytes 12532
  1.4 32.7 %copy-start.5 = (f32[72]{0:T(128)S(1)}, f32[72]{0:T(128)}, u32[]{:S(2)}) copy-start(f32[72]{0:T(128)} %mix_ref.1) | copy-start | bytes 868
  6.6 29.5 %all-to-all-start = ((bf16[24,24,128]{2,1,0:T(8,128)(2,1)}), bf16[24,24,128]{2,1,0:T(8,128)(2,1)S(1)}, u32[]{:S(2)}, u32[]{:S(2)}) async-start(bf16[24,24,128]{2,1,0:T(8,128)(2,1)} %get-tuple-element.15), calls=%async_computation | async-start | bytes 294912 | tf_op jit(solution)/shard_map/all_to_all | solution.py:417
  23.5 30.2 %collective-permute-start.1 = (bf16[1044,128]{1,0:T(8,128)(2,1)S(1)}, bf16[1044,128]{1,0:T(8,128)(2,1)S(1)}, u32[]{:S(2)}, u32[]{:S(2)}) collective-permute-start(bf16[1044,128]{1,0:T(8,128)(2,1)S(1)} %copy-done), channel_id=1, source_target_pairs={{0,1},{1,2},{2,3},{3,4},{4,5},{5,6},{6,7},{7,8},{8,9},{9,10},{10,1... | collective-permute-start | bytes 801800 | tf_op jit(solution)/shard_map/ppermute | solution.py:433
  26.7 27.0 %collective-permute-start.2 = (bf16[1044,128]{1,0:T(8,128)(2,1)S(1)}, bf16[1044,128]{1,0:T(8,128)(2,1)S(1)}, u32[]{:S(2)}, u32[]{:S(2)}) collective-permute-start(bf16[1044,128]{1,0:T(8,128)(2,1)S(1)} %copy-done), channel_id=1, source_target_pairs={{1,0},{2,1},{3,2},{4,3},{5,4},{6,5},{7,6},{8,7},{9,8},{10,9},{11,1... | collective-permute-start | bytes 801800 | tf_op jit(solution)/shard_map/ppermute | solution.py:434
  36.1 4.1 %collective-permute-start = (bf16[24,24,128]{2,1,0:T(8,128)(2,1)S(1)}, bf16[24,24,128]{2,1,0:T(8,128)(2,1)S(1)}, u32[]{:S(2)}, u32[]{:S(2)}) collective-permute-start(bf16[24,24,128]{2,1,0:T(8,128)(2,1)S(1)} %all-to-all-done.own_ref), channel_id=1, source_target_pairs={{0,16},{16,0},{32,48},{48,32},{64,80},{80,64},{96,112},{112,96},{1... | collective-permute-start | bytes 442376 | tf_op jit(solution)/shard_map/ppermute | solution.py:420
  40.2 13.5 %copy-start.3 = (s32[512]{0:T(512)S(1)}, s32[512]{0:T(512)}, u32[]{:S(2)}) copy-start(s32[512]{0:T(512)} %param.22) | copy-start | bytes 6148
  40.2 13.5 %copy-start.4 = (s32[512]{0:T(512)S(1)}, s32[512]{0:T(512)}, u32[]{:S(2)}) copy-start(s32[512]{0:T(512)} %param.23) | copy-start | bytes 6148
  44.9 17.5 %all-to-all-start.1 = ((f32[16,1,128]{2,1,0:T(1,128)}), f32[16,1,128]{2,1,0:T(1,128)S(1)}, u32[]{:S(2)}, u32[]{:S(2)}) async-start(f32[16,1,128]{2,1,0:T(1,128)} %bitcast.3), calls=%async_computation.1 | async-start | bytes 16384 | tf_op jit(solution)/shard_map/all_to_all | solution.py:448
  97.7 12.9 %all-to-all-start.3 = ((bf16[16,40,128]{2,1,0:T(8,128)(2,1)}), bf16[16,40,128]{2,1,0:T(8,128)(2,1)S(1)}, u32[]{:S(2)}, u32[]{:S(2)}) async-start(bf16[16,40,128]{2,1,0:T(8,128)(2,1)} %scatter.1), calls=%async_computation.3 | async-start | bytes 327680 | tf_op jit(solution)/shard_map/all_to_all | solution.py:511

commit v4 on v3

--- a/solution.py
+++ b/solution.py
@@ -389,27 +389,29 @@
     fld = lax.axis_index("fld")
     shape = jax.ShapeDtypeStruct
 
-    per = 4
+    per = slots // 2
     wave_row = wave_slot[None, :]
     sums, packed = pl.pallas_call(
         functools.partial(legendre_kernel, per, slots),
-        grid=(slots // per,),
-        in_specs=[
-            SMEM,
-            pl.BlockSpec((per, lats, degrees), lambda i: (i, 0, 0)),
-            pl.BlockSpec((per, 2 * levels, degrees), lambda i: (i, 0, 0)),
-        ],
-        out_specs=[
-            pl.BlockSpec((lats * slots, 2 * levels), lambda i: (0, 0)),
-            pl.BlockSpec((owners // 2, 24, LANES), lambda i: (0, 0, 0)),
-        ],
+        grid_spec=pltpu.PrefetchScalarGridSpec(
+            num_scalar_prefetch=1,
+            grid=(slots // per,),
+            in_specs=[
+                pl.BlockSpec((per, lats, degrees), lambda i, _: (i, 0, 0)),
+                pl.BlockSpec((per, 2 * levels, degrees), lambda i, _: (i, 0, 0)),
+            ],
+            out_specs=[
+                pl.BlockSpec((lats * slots, 2 * levels), lambda i, _: (0, 0)),
+                pl.BlockSpec((owners // 2, 24, LANES), lambda i, _: (0, 0, 0)),
+            ],
+            scratch_shapes=[
+                pltpu.VMEM((lats * slots, LANES), f32),
+                pltpu.VMEM((lats * slots, LANES), f32),
+                pltpu.VMEM((LANES, LANES), f32),
+            ],
+        ),
         out_shape=[shape((lats * slots, 2 * levels), bf16), shape((owners // 2, 24, LANES), bf16)],
-        scratch_shapes=[
-            pltpu.VMEM((lats * slots, LANES), f32),
-            pltpu.VMEM((lats * slots, LANES), f32),
-            pltpu.VMEM((LANES, LANES), f32),
-        ],
-        compiler_params=params(53),
+        compiler_params=params(54),
         cost_estimate=cost(3e8, 5e6),
         name="legendre",
     )(wave_slot, legendre, spectral.reshape(slots, 2 * levels, degrees))
@@ -465,7 +467,7 @@
         compiler_params=params(10),
         cost_estimate=cost(2e8, 2e6),
         name="mix",
-    )(mixing, sums, codes)
+    )(mixing, after(sums, picked), codes)
 
     adv, base = pl.pallas_call(
         advect_kernel,

time: 113 us -> 112 us (level)
  starting transfers between devices: 42.2 us -> 46.2 us
  waiting for transfers between devices: 10.8 us -> 8.55 us
  blocking collectives: 32.9 us -> 30.9 us
    all_to_all x1, blocking collectives: 32.9 us -> 30.9 us  [local(): lax.all_to_all(outgoing, 'lat', split_axis=0, concat_axis=0, tiled=True)]
    all_to_all x1, waiting for transfers between devices: 5.44 us -> 3.37 us  [local(): lax.all_to_all(picked, 'fld', split_axis=0, concat_axis=0, tiled=True)]
    ppermute x1, starting transfers between devices: 3.08 us -> 5.02 us  [local(): lax.ppermute(own_part, 'lat', [(k, k ^ 1) for k in range(owners)])]
    all_to_all x1, starting transfers between devices: 3.52 us -> 5.43 us  [local(): lax.all_to_all(partial, 'fld', split_axis=0, concat_axis=0, tiled=True)]
  transfers between devices with their start and end apart: 6 -> 6, of which waited for: 2 -> 3; matrix products, arithmetic and copies ran while one was open for 0% -> 0% of each run, Pallas kernels for 13% -> 13%
where the time goes in v4:
time: 112 us; the launch traced here: 111 us
  starting transfers between devices  46.2 us (41%)
  blocking collectives  30.9 us (28%)
  Pallas kernels  23.3 us (21%)
  waiting for transfers between devices  8.55 us (8%)
  between operations  1.55 us (1%)
    all_to_all x1, blocking collectives, local(): lax.all_to_all(outgoing, 'lat', split_axis=0, concat_axis=0, tiled=True)  30.9 us
    all_to_all x1, starting transfers between devices, local(): lax.all_to_all(packed, 'lat', split_axis=0, concat_axis=0, tiled=True, ax...  16.9 us
    all_to_all x1, starting transfers between devices, local(): lax.all_to_all(picked, 'fld', split_axis=0, concat_axis=0, tiled=True)  8.91 us
    ppermute x1, starting transfers between devices, local(): high = lax.ppermute(wave_state, ('lat', 'fld'), [(b, a) for a, b in up])  6.82 us
    pallas_call x1, Pallas kernels, local(): pl.pallas_call(functools.partial(legendre_kernel, per, slots), grid_spec=...  5.44 us
    all_to_all x1, starting transfers between devices, local(): lax.all_to_all(partial, 'fld', split_axis=0, concat_axis=0, tiled=True)  5.43 us
    all_to_all x1, waiting for transfers between devices, local(): lax.all_to_all(partial, 'fld', split_axis=0, concat_axis=0, tiled=True)  5.04 us
    ppermute x1, starting transfers between devices, local(): lax.ppermute(own_part, 'lat', [(k, k ^ 1) for k in range(owners)])  5.02 us
  transfers between devices with their start and end apart: 6, of which 3 were waited for; matrix products, arithmetic and copies ran while one was open for 0% of the time, Pallas kernels for 13%

profile of v4, /device:TPU:1, one launch (start us, length us, event | category | flops | bytes accessed | tf_op | source)
XLA Modules:
  0.0 111.0 jit_solution(2953737411900756915)
XLA Ops:
  0.6 0.0 copy-start.1
  0.6 0.0 copy-start.6
  0.7 0.0 copy-start.7
  0.7 0.0 copy-start.8
  0.7 0.0 copy-start.5
  0.7 0.0 copy-start.9
  0.7 5.4 %legendre.1 = (bf16[1536,144]{1,0:T(8,128)(2,1)}, bf16[24,24,128]{2,1,0:T(8,128)(2,1)}) custom-call(s32[768]{0:T(1024)} %wave_ref.1, bf16[16,96,640]{2,1,0:T(8,128)(2,1)} %leg_ref.1, bf16[16,144,640]{2,1,0:T(8,128)(2,1)} %bitcast.16), custom_call_target="tpu_custom_call" | custom-call | flops 300000000 | bytes 5000000 | tf_op jit(solution)/shard_map/legendre/pallas_call | solution.py:394
  6.1 16.9 %all-to-all-start = ((bf16[24,24,128]{2,1,0:T(8,128)(2,1)}), bf16[24,24,128]{2,1,0:T(8,128)(2,1)S(1)}, u32[]{:S(2)}, u32[]{:S(2)}) async-start(bf16[24,24,128]{2,1,0:T(8,128)(2,1)} %get-tuple-element.16), calls=%async_computation | async-start | bytes 294912 | tf_op jit(solution)/shard_map/all_to_all | solution.py:419
  23.0 0.0 copy-done.1
  23.0 3.2 %collective-permute-start.1 = (bf16[1044,128]{1,0:T(8,128)(2,1)S(1)}, bf16[1044,128]{1,0:T(8,128)(2,1)S(1)}, u32[]{:S(2)}, u32[]{:S(2)}) collective-permute-start(bf16[1044,128]{1,0:T(8,128)(2,1)S(1)} %copy-done.1), channel_id=1, source_target_pairs={{0,1},{1,2},{2,3},{3,4},{4,5},{5,6},{6,7},{7,8},{8,9},{9,10},{10,1... | collective-permute-start | bytes 801800 | tf_op jit(solution)/shard_map/ppermute | solution.py:435
  26.2 6.8 %collective-permute-start.2 = (bf16[1044,128]{1,0:T(8,128)(2,1)S(1)}, bf16[1044,128]{1,0:T(8,128)(2,1)S(1)}, u32[]{:S(2)}, u32[]{:S(2)}) collective-permute-start(bf16[1044,128]{1,0:T(8,128)(2,1)S(1)} %copy-done.1), channel_id=1, source_target_pairs={{1,0},{2,1},{3,2},{4,3},{5,4},{6,5},{7,6},{8,7},{9,8},{10,9},{11,1... | collective-permute-start | bytes 801800 | tf_op jit(solution)/shard_map/ppermute | solution.py:436
  33.0 0.0 copy-done.6
  33.1 0.0 copy-done.7
  33.1 0.1 multiply_bitcast_fusion.1
  33.2 0.1 convert_element_type.10
  33.3 0.0 copy-done.8
  33.3 0.0 copy-done.5
  33.3 0.2 copy.17.coupling_ref
  33.5 0.0 copy-done.9
  33.5 0.1 pad.4.codes_ref
  33.6 0.1 all-to-all-done.own_ref
  33.7 5.0 %collective-permute-start = (bf16[24,24,128]{2,1,0:T(8,128)(2,1)S(1)}, bf16[24,24,128]{2,1,0:T(8,128)(2,1)S(1)}, u32[]{:S(2)}, u32[]{:S(2)}) collective-permute-start(bf16[24,24,128]{2,1,0:T(8,128)(2,1)S(1)} %all-to-all-done.own_ref), channel_id=1, source_target_pairs={{0,16},{16,0},{32,48},{48,32},{64,80},{80,64},{96,112},{112,96},{1... | collective-permute-start | bytes 442376 | tf_op jit(solution)/shard_map/ppermute | solution.py:422
  38.7 1.0 long.1.long_ref
  39.7 0.0 copy-start.2
  39.7 0.0 copy-start.3
  39.7 0.0 collective-permute-done.other_ref
  39.8 4.6 %surface.1 = f32[16,128]{1,0:T(8,128)} custom-call(bf16[24,24,128]{2,1,0:T(8,128)(2,1)S(1)} %all-to-all-done.own_ref, bf16[24,24,128]{2,1,0:T(8,128)(2,1)S(1)} %collective-permute-done.other_ref, bf16[640,1536]{1,0:T(8,128)(2,1)S(1)} %long.1.long_ref, s32[1,768]{1,0:T(1,128)S(1)} %broadcast_in_dim.15.wave_ref, s32[2048]{0:T(1024)S(1)} %get-tuple-element.33.row_ref, ...), custom_call_target="tpu_custom_call" | custom-call | flops 1000000000 | bytes 4000000 | tf_op jit(solution)/shard_map/surface/pallas_call | solution.py:440
  44.4 0.0 copy-start
  44.4 0.0 copy-start.4
  44.4 8.9 %all-to-all-start.1 = ((f32[16,1,128]{2,1,0:T(1,128)}), f32[16,1,128]{2,1,0:T(1,128)S(1)}, u32[]{:S(2)}, u32[]{:S(2)}) async-start(f32[16,1,128]{2,1,0:T(1,128)} %bitcast.3), calls=%async_computation.1 | async-start | bytes 16384 | tf_op jit(solution)/shard_map/all_to_all | solution.py:450
  53.3 0.0 collective-permute-done.1.low_ref
  53.3 0.0 collective-permute-done.2.high_ref
  53.3 0.0 copy-done.2
  53.4 0.0 copy-done.3
  53.4 3.2 %advect.1 = (f32[1044,128]{1,0:T(8,128)S(1)}, f32[1044,128]{1,0:T(8,128)S(1)}) custom-call(bf16[1044,128]{1,0:T(8,128)(2,1)S(1)} %copy-done.1, bf16[1044,128]{1,0:T(8,128)(2,1)S(1)} %collective-permute-done.1.low_ref, bf16[1044,128]{1,0:T(8,128)(2,1)S(1)} %collective-permute-done.2.high_ref, s32[1,512]{1,0:T(1,128)S(1)} %bitcast.14, s32[1,512]{1,0:T(1,128)S(1)} %bitcast.15, ...), custom_call_target="tpu_custom_call" | custom-call | flops 500000000 | bytes 4000000 | tf_op jit(solution)/shard_map/advect/pallas_call | solution.py:472
  56.6 0.0 copy-done
  56.6 0.0 copy-done.4
  56.6 2.0 %mix.1 = (bf16[48,32,128]{2,1,0:T(8,128)(2,1)S(1)}, f32[48,8,128]{2,1,0:T(8,128)S(1)}, f32[72,128]{1,0:T(8,128)S(1)}) custom-call(f32[72]{0:T(128)S(1)} %copy-done.4, bf16[1536,144]{1,0:T(8,128)(2,1)S(1)} %copy-done, f32[8,128]{1,0:T(8,128)S(1)} %pad.4.codes_ref), custom_call_target="tpu_custom_call" | custom-call | flops 200000000 | bytes 2000000 | tf_op jit(solution)/shard_map/mix/pallas_call | solution.py:457
  58.7 3.4 %all-to-all-done.1 = f32[16,1,128]{2,1,0:T(1,128)S(1)} async-done(((f32[16,1,128]{2,1,0:T(1,128)}), f32[16,1,128]{2,1,0:T(1,128)S(1)}, u32[]{:S(2)}, u32[]{:S(2)}) %all-to-all-start.1) | async-done | bytes 8224 | tf_op jit(solution)/shard_map/all_to_all | solution.py:450
  62.1 1.0 wave.1
  63.0 30.9 %all_to_all.26.y_ref = bf16[48,40,128]{2,1,0:T(8,128)(2,1)S(1)} all-to-all(bf16[48,40,128]{2,1,0:T(8,128)(2,1)S(1)} %get-tuple-element.25), channel_id=1, replica_groups=mesh['lat'=48,'fld'=16] {'lat'}, dimensions={0} | all-to-all | bytes 983040 | tf_op jit(solution)/shard_map/all_to_all | solution.py:500
  93.9 1.4 %scatter.1 = bf16[16,40,128]{2,1,0:T(8,128)(2,1)} custom-call(bf16[48,40,128]{2,1,0:T(8,128)(2,1)S(1)} %all_to_all.26.y_ref), custom_call_target="tpu_custom_call" | custom-call | flops 100000000 | bytes 2000000 | tf_op jit(solution)/shard_map/scatter/pallas_call | solution.py:503
  95.3 5.4 %all-to-all-start.3 = ((bf16[16,40,128]{2,1,0:T(8,128)(2,1)}), bf16[16,40,128]{2,1,0:T(8,128)(2,1)S(1)}, u32[]{:S(2)}, u32[]{:S(2)}) async-start(bf16[16,40,128]{2,1,0:T(8,128)(2,1)} %scatter.1), calls=%async_computation.3 | async-start | bytes 327680 | tf_op jit(solution)/shard_map/all_to_all | solution.py:513
  101.4 1.4 %wide.1.wide_ref = bf16[1536,640]{1,0:T(8,128)(2,1)S(1)} custom-call(s32[1,768]{1,0:T(1,128)S(1)} %broadcast_in_dim.15.wave_ref), custom_call_target="tpu_custom_call" | custom-call | flops 6000000 | bytes 3000000 | tf_op jit(solution)/shard_map/wide/pallas_call | solution.py:516
  102.8 2.0 %synthesis.1.d_ref = bf16[2,72,2560]{2,1,0:T(8,128)(2,1)S(1)} custom-call(bf16[48,40,128]{2,1,0:T(8,128)(2,1)S(1)} %all_to_all.26.y_ref, s32[1,768]{1,0:T(1,128)S(1)} %broadcast_in_dim.15.wave_ref, bf16[1536,640]{1,0:T(8,128)(2,1)S(1)} %wide.1.wide_ref), custom_call_target="tpu_custom_call" | custom-call | flops 1200000000 | bytes 6000000 | tf_op jit(solution)/shard_map/synthesis/pallas_call | solution.py:525
  104.8 5.0 %all-to-all-done.3.part_ref = bf16[16,40,128]{2,1,0:T(8,128)(2,1)S(1)} async-done(((bf16[16,40,128]{2,1,0:T(8,128)(2,1)}), bf16[16,40,128]{2,1,0:T(8,128)(2,1)S(1)}, u32[]{:S(2)}, u32[]{:S(2)}) %all-to-all-start.3) | async-done | bytes 163872 | tf_op jit(solution)/shard_map/all_to_all | solution.py:513
  109.8 1.1 %final.1 = bf16[2,1,72,2560]{3,2,1,0:T(8,128)(2,1)} custom-call(bf16[2,72,2560]{2,1,0:T(8,128)(2,1)S(1)} %synthesis.1.d_ref, bf16[16,40,128]{2,1,0:T(8,128)(2,1)S(1)} %all-to-all-done.3.part_ref, f32[72,128]{1,0:T(8,128)S(1)} %get-tuple-element.28.col_ref, f32[1]{0:T(128)S(6)} %copy.18.drag_ref), custom_call_target="tpu_custom_call" | custom-call | flops 1000000 | bytes 3000000 | tf_op jit(solution)/shard_map/final/pallas_call | solution.py:536
  (5 shorter events, 0.0 us)
Async XLA Ops:
  0.6 22.4 %copy-start.1 = (bf16[1044,128]{1,0:T(8,128)(2,1)S(1)}, bf16[1044,128]{1,0:T(8,128)(2,1)}, u32[]{:S(2)}) copy-start(bf16[1044,128]{1,0:T(8,128)(2,1)} %state_ref.1) | copy-start | bytes 801796
  0.6 32.4 %copy-start.6 = (s32[768]{0:T(1024)S(1)}, s32[768]{0:T(1024)}, u32[]{:S(2)}) copy-start(s32[768]{0:T(1024)} %wave_ref.1) | copy-start | bytes 9220
  0.7 32.4 %copy-start.7 = (s32[2048]{0:T(1024)S(1)}, s32[2048]{0:T(1024)}, u32[]{:S(2)}) copy-start(s32[2048]{0:T(1024)} %param.21) | copy-start | bytes 24580
  0.7 32.6 %copy-start.8 = (f32[1044]{0:T(1024)S(1)}, f32[1044]{0:T(1024)}, u32[]{:S(2)}) copy-start(f32[1044]{0:T(1024)} %param.18) | copy-start | bytes 12532
  0.7 32.6 %copy-start.5 = (bf16[1044,16]{0,1:T(8,128)(2,1)S(1)}, bf16[1044,16]{0,1:T(8,128)(2,1)}, u32[]{:S(2)}) copy-start(bf16[1044,16]{0,1:T(8,128)(2,1)} %param.16) | copy-start | bytes 100228
  0.7 32.8 %copy-start.9 = (f32[1044]{0:T(1024)S(1)}, f32[1044]{0:T(1024)}, u32[]{:S(2)}) copy-start(f32[1044]{0:T(1024)} %param.19) | copy-start | bytes 12532
  6.1 27.6 %all-to-all-start = ((bf16[24,24,128]{2,1,0:T(8,128)(2,1)}), bf16[24,24,128]{2,1,0:T(8,128)(2,1)S(1)}, u32[]{:S(2)}, u32[]{:S(2)}) async-start(bf16[24,24,128]{2,1,0:T(8,128)(2,1)} %get-tuple-element.16), calls=%async_computation | async-start | bytes 294912 | tf_op jit(solution)/shard_map/all_to_all | solution.py:419
  23.0 30.3 %collective-permute-start.1 = (bf16[1044,128]{1,0:T(8,128)(2,1)S(1)}, bf16[1044,128]{1,0:T(8,128)(2,1)S(1)}, u32[]{:S(2)}, u32[]{:S(2)}) collective-permute-start(bf16[1044,128]{1,0:T(8,128)(2,1)S(1)} %copy-done.1), channel_id=1, source_target_pairs={{0,1},{1,2},{2,3},{3,4},{4,5},{5,6},{6,7},{7,8},{8,9},{9,10},{10,1... | collective-permute-start | bytes 801800 | tf_op jit(solution)/shard_map/ppermute | solution.py:435
  26.2 27.1 %collective-permute-start.2 = (bf16[1044,128]{1,0:T(8,128)(2,1)S(1)}, bf16[1044,128]{1,0:T(8,128)(2,1)S(1)}, u32[]{:S(2)}, u32[]{:S(2)}) collective-permute-start(bf16[1044,128]{1,0:T(8,128)(2,1)S(1)} %copy-done.1), channel_id=1, source_target_pairs={{1,0},{2,1},{3,2},{4,3},{5,4},{6,5},{7,6},{8,7},{9,8},{10,9},{11,1... | collective-permute-start | bytes 801800 | tf_op jit(solution)/shard_map/ppermute | solution.py:436
  33.7 6.1 %collective-permute-start = (bf16[24,24,128]{2,1,0:T(8,128)(2,1)S(1)}, bf16[24,24,128]{2,1,0:T(8,128)(2,1)S(1)}, u32[]{:S(2)}, u32[]{:S(2)}) collective-permute-start(bf16[24,24,128]{2,1,0:T(8,128)(2,1)S(1)} %all-to-all-done.own_ref), channel_id=1, source_target_pairs={{0,16},{16,0},{32,48},{48,32},{64,80},{80,64},{96,112},{112,96},{1... | collective-permute-start | bytes 442376 | tf_op jit(solution)/shard_map/ppermute | solution.py:422
  39.7 13.6 %copy-start.2 = (s32[512]{0:T(512)S(1)}, s32[512]{0:T(512)}, u32[]{:S(2)}) copy-start(s32[512]{0:T(512)} %param.22) | copy-start | bytes 6148
  39.7 13.6 %copy-start.3 = (s32[512]{0:T(512)S(1)}, s32[512]{0:T(512)}, u32[]{:S(2)}) copy-start(s32[512]{0:T(512)} %param.23) | copy-start | bytes 6148
  44.4 12.2 %copy-start = (bf16[1536,144]{1,0:T(8,128)(2,1)S(1)}, bf16[1536,144]{1,0:T(8,128)(2,1)}, u32[]{:S(2)}) copy-start(bf16[1536,144]{1,0:T(8,128)(2,1)} %get-tuple-element.22.f_ref) | copy-start | bytes 1327108
  44.4 12.2 %copy-start.4 = (f32[72]{0:T(128)S(1)}, f32[72]{0:T(128)}, u32[]{:S(2)}) copy-start(f32[72]{0:T(128)} %mix_ref.1) | copy-start | bytes 868
  44.4 17.6 %all-to-all-start.1 = ((f32[16,1,128]{2,1,0:T(1,128)}), f32[16,1,128]{2,1,0:T(1,128)S(1)}, u32[]{:S(2)}, u32[]{:S(2)}) async-start(f32[16,1,128]{2,1,0:T(1,128)} %bitcast.3), calls=%async_computation.1 | async-start | bytes 16384 | tf_op jit(solution)/shard_map/all_to_all | solution.py:450
  95.3 14.5 %all-to-all-start.3 = ((bf16[16,40,128]{2,1,0:T(8,128)(2,1)}), bf16[16,40,128]{2,1,0:T(8,128)(2,1)S(1)}, u32[]{:S(2)}, u32[]{:S(2)}) async-start(bf16[16,40,128]{2,1,0:T(8,128)(2,1)} %scatter.1), calls=%async_computation.3 | async-start | bytes 327680 | tf_op jit(solution)/shard_map/all_to_all | solution.py:513

commit v5 on v4

--- a/solution.py
+++ b/solution.py
@@ -203,11 +203,8 @@
 
 
 def surface_kernel(slots, own_ref, other_ref, long_ref, wave_ref, row_ref, lat_ref, o_ref, surface, picked):
-    first = lax.rem(lax.axis_index("lat"), 2) == 0
-    own, other = unpacked(own_ref), unpacked(other_ref)
     real, imaginary = [
-        jnp.stack([jnp.where(first, a, b), jnp.where(first, b, a)], axis=1).reshape(slots, LANES)
-        for a, b in zip(own, other)
+        jnp.concatenate([a, b], axis=0).reshape(slots, LANES) for a, b in zip(unpacked(own_ref), unpacked(other_ref))
     ]
     pairs = turned(real, imaginary, [upright(x) for x in quarters(wave_ref[...])])
     coefficients = jnp.concatenate(
@@ -420,6 +417,8 @@
         packed, "lat", split_axis=0, concat_axis=0, tiled=True, axis_index_groups=same_core
     )
     other_part = lax.ppermute(own_part, "lat", [(k, k ^ 1) for k in range(owners)])
+    by_core = wave_slot.reshape(owners // 2, 2, slots).transpose(1, 0, 2).reshape(2, all_slots // 2)
+    by_core = jnp.where(lax.axis_index("lat") % 2 == 0, by_core, by_core[::-1]).reshape(1, all_slots)
     long = pl.pallas_call(
         long_kernel,
         in_specs=[VMEM],
@@ -428,7 +427,7 @@
         compiler_params=params(10),
         cost_estimate=cost(6e6, 3e6),
         name="long",
-    )(after(wave_row, own_part))
+    )(after(by_core, own_part))
 
     tiles = owners * columns
     up = [(k, k + 1) for k in range(tiles - 1)]
@@ -446,7 +445,7 @@
         compiler_params=params(14),
         cost_estimate=cost(1e9, 4e6),
         name="surface",
-    )(own_part, other_part, long, wave_row, rows, lat_row.reshape(columns, points))
+    )(own_part, other_part, long, by_core, rows, lat_row.reshape(columns, points))
     forcing = lax.all_to_all(picked, "fld", split_axis=0, concat_axis=0, tiled=True)
 
     own_cells = lax.dynamic_slice_in_dim(cell_index, fld * points, points)

time: 112 us -> 117 us (1.045)
  waiting for transfers between devices: 8.55 us -> 18.3 us
  starting transfers between devices: 46.2 us -> 42.2 us
    all_to_all x1, waiting for transfers between devices: 0.13 us -> 9.81 us  [local(): lax.all_to_all(packed, 'lat', split_axis=0, concat_axis=0, tiled=True, ax...]
    all_to_all x1, starting transfers between devices: 8.91 us -> 6.4 us  [local(): lax.all_to_all(picked, 'fld', split_axis=0, concat_axis=0, tiled=True)]
    all_to_all x1, starting transfers between devices: 16.9 us -> 15.2 us  [local(): lax.all_to_all(packed, 'lat', split_axis=0, concat_axis=0, tiled=True, ax...]
  transfers between devices with their start and end apart: 6 -> 6, of which waited for: 3 -> 3; matrix products, arithmetic and copies ran while one was open for 0% -> 1% of each run, Pallas kernels for 13% -> 17%
where the time goes in v5:
time: 117 us; the launch traced here: 116 us
  starting transfers between devices  42.2 us (36%)
  blocking collectives  29.9 us (26%)
  Pallas kernels  23.2 us (20%)
  waiting for transfers between devices  18.3 us (16%)
  between operations  1.62 us (1%)
    all_to_all x1, blocking collectives, local(): lax.all_to_all(outgoing, 'lat', split_axis=0, concat_axis=0, tiled=True)  29.9 us
    all_to_all x1, starting transfers between devices, local(): lax.all_to_all(packed, 'lat', split_axis=0, concat_axis=0, tiled=True, ax...  15.2 us
    all_to_all x1, waiting for transfers between devices, local(): lax.all_to_all(packed, 'lat', split_axis=0, concat_axis=0, tiled=True, ax...  9.81 us
    ppermute x1, starting transfers between devices, local(): high = lax.ppermute(wave_state, ('lat', 'fld'), [(b, a) for a, b in up])  6.84 us
    all_to_all x1, starting transfers between devices, local(): lax.all_to_all(picked, 'fld', split_axis=0, concat_axis=0, tiled=True)  6.4 us
    pallas_call x1, Pallas kernels, local(): pl.pallas_call(functools.partial(legendre_kernel, per, slots), grid_spec=...  5.44 us
    all_to_all x1, waiting for transfers between devices, local(): lax.all_to_all(partial, 'fld', split_axis=0, concat_axis=0, tiled=True)  5.08 us
    ppermute x1, starting transfers between devices, local(): lax.ppermute(own_part, 'lat', [(k, k ^ 1) for k in range(owners)])  4.91 us
  transfers between devices with their start and end apart: 6, of which 3 were waited for; matrix products, arithmetic and copies ran while one was open for 1% of the time, Pallas kernels for 17%

profile of v5, /device:TPU:1, one launch (start us, length us, event | category | flops | bytes accessed | tf_op | source)
XLA Modules:
  0.0 115.9 jit_solution(17540432219443190824)
XLA Ops:
  0.6 4.0 %collective-permute-start.1 = (bf16[1044,128]{1,0:T(8,128)(2,1)}, bf16[1044,128]{1,0:T(8,128)(2,1)S(1)}, u32[]{:S(2)}, u32[]{:S(2)}) collective-permute-start(bf16[1044,128]{1,0:T(8,128)(2,1)} %state_ref.1), channel_id=1, source_target_pairs={{0,1},{1,2},{2,3},{3,4},{4,5},{5,6},{6,7},{7,8},{8,9},{9,10},{10,1... | collective-permute-start | bytes 801800 | tf_op jit(solution)/shard_map/ppermute | solution.py:434
  4.7 6.8 %collective-permute-start.2 = (bf16[1044,128]{1,0:T(8,128)(2,1)}, bf16[1044,128]{1,0:T(8,128)(2,1)S(1)}, u32[]{:S(2)}, u32[]{:S(2)}) collective-permute-start(bf16[1044,128]{1,0:T(8,128)(2,1)} %state_ref.1), channel_id=1, source_target_pairs={{1,0},{2,1},{3,2},{4,3},{5,4},{6,5},{7,6},{8,7},{9,8},{10,9},{11,1... | collective-permute-start | bytes 801800 | tf_op jit(solution)/shard_map/ppermute | solution.py:435
  11.5 0.0 copy-start.6
  11.5 0.0 copy-start.8
  11.5 0.0 copy-start.7
  11.5 0.0 copy-start.5
  11.6 0.0 copy-start.9
  11.6 5.4 %legendre.1 = (bf16[1536,144]{1,0:T(8,128)(2,1)}, bf16[24,24,128]{2,1,0:T(8,128)(2,1)}) custom-call(s32[768]{0:T(1024)} %wave_ref.1, bf16[16,96,640]{2,1,0:T(8,128)(2,1)} %leg_ref.1, bf16[16,144,640]{2,1,0:T(8,128)(2,1)} %bitcast.23), custom_call_target="tpu_custom_call" | custom-call | flops 300000000 | bytes 5000000 | tf_op jit(solution)/shard_map/legendre/pallas_call | solution.py:391
  17.0 15.2 %all-to-all-start = ((bf16[24,24,128]{2,1,0:T(8,128)(2,1)}), bf16[24,24,128]{2,1,0:T(8,128)(2,1)S(1)}, u32[]{:S(2)}, u32[]{:S(2)}) async-start(bf16[24,24,128]{2,1,0:T(8,128)(2,1)} %get-tuple-element.16), calls=%async_computation | async-start | bytes 294912 | tf_op jit(solution)/shard_map/all_to_all | solution.py:416
  32.2 0.0 copy-done.6
  32.2 0.1 reshape.25
  32.3 0.1 reshape.26
  32.4 0.1 rev.3
  32.5 0.0 copy-done.8
  32.6 0.0 copy-done.7
  32.6 0.1 multiply_bitcast_fusion.1
  32.7 0.1 convert_element_type.10
  32.8 0.0 copy-done.5
  32.8 0.2 copy.20.coupling_ref
  33.0 0.0 copy-done.9
  33.0 0.1 pad.4.codes_ref
  33.1 9.8 %all-to-all-done.own_ref = bf16[24,24,128]{2,1,0:T(8,128)(2,1)S(1)} async-done(((bf16[24,24,128]{2,1,0:T(8,128)(2,1)}), bf16[24,24,128]{2,1,0:T(8,128)(2,1)S(1)}, u32[]{:S(2)}, u32[]{:S(2)}) %all-to-all-start) | async-done | bytes 147488 | tf_op jit(solution)/shard_map/all_to_all | solution.py:416
  42.9 4.9 %collective-permute-start = (bf16[24,24,128]{2,1,0:T(8,128)(2,1)S(1)}, bf16[24,24,128]{2,1,0:T(8,128)(2,1)S(1)}, u32[]{:S(2)}, u32[]{:S(2)}) collective-permute-start(bf16[24,24,128]{2,1,0:T(8,128)(2,1)S(1)} %all-to-all-done.own_ref), channel_id=1, source_target_pairs={{0,16},{16,0},{32,48},{48,32},{64,80},{80,64},{96,112},{112,96},{1... | collective-permute-start | bytes 442376 | tf_op jit(solution)/shard_map/ppermute | solution.py:419
  47.8 1.0 long.1.long_ref
  48.8 0.0 copy-start.1
  48.8 0.0 copy-start.2
  48.8 0.0 copy-start.3
  48.8 0.0 collective-permute-done.other_ref
  48.9 4.6 %surface.1 = f32[16,128]{1,0:T(8,128)} custom-call(bf16[24,24,128]{2,1,0:T(8,128)(2,1)S(1)} %all-to-all-done.own_ref, bf16[24,24,128]{2,1,0:T(8,128)(2,1)S(1)} %collective-permute-done.other_ref, bf16[640,1536]{1,0:T(8,128)(2,1)S(1)} %long.1.long_ref, s32[1,768]{1,0:T(1,128)S(1)} %bitcast.20, s32[2048]{0:T(1024)S(1)} %get-tuple-element.33.row_ref, ...), custom_call_target="tpu_custom_call" | custom-call | flops 1000000000 | bytes 4000000 | tf_op jit(solution)/shard_map/surface/pallas_call | solution.py:439
  53.5 6.4 %all-to-all-start.1 = ((f32[16,1,128]{2,1,0:T(1,128)}), f32[16,1,128]{2,1,0:T(1,128)S(1)}, u32[]{:S(2)}, u32[]{:S(2)}) async-start(f32[16,1,128]{2,1,0:T(1,128)} %bitcast.4), calls=%async_computation.1 | async-start | bytes 16384 | tf_op jit(solution)/shard_map/all_to_all | solution.py:449
  59.9 0.0 collective-permute-done.1.low_ref
  59.9 0.0 collective-permute-done.2.high_ref
  59.9 0.0 copy-done.1
  59.9 0.0 copy-done.2
  59.9 0.0 copy-done.3
  59.9 3.2 %advect.1 = (f32[1044,128]{1,0:T(8,128)S(1)}, f32[1044,128]{1,0:T(8,128)S(1)}) custom-call(bf16[1044,128]{1,0:T(8,128)(2,1)S(1)} %copy-done.1, bf16[1044,128]{1,0:T(8,128)(2,1)S(1)} %collective-permute-done.1.low_ref, bf16[1044,128]{1,0:T(8,128)(2,1)S(1)} %collective-permute-done.2.high_ref, s32[1,512]{1,0:T(1,128)S(1)} %bitcast.21, s32[1,512]{1,0:T(1,128)S(1)} %bitcast.22, ...), custom_call_target="tpu_custom_call" | custom-call | flops 500000000 | bytes 4000000 | tf_op jit(solution)/shard_map/advect/pallas_call | solution.py:471
  63.2 0.0 copy-done
  63.2 0.0 copy-done.4
  63.2 2.0 %mix.1 = (bf16[48,32,128]{2,1,0:T(8,128)(2,1)S(1)}, f32[48,8,128]{2,1,0:T(8,128)S(1)}, f32[72,128]{1,0:T(8,128)S(1)}) custom-call(f32[72]{0:T(128)S(1)} %copy-done.4, bf16[1536,144]{1,0:T(8,128)(2,1)S(1)} %copy-done, f32[8,128]{1,0:T(8,128)S(1)} %pad.4.codes_ref), custom_call_target="tpu_custom_call" | custom-call | flops 200000000 | bytes 2000000 | tf_op jit(solution)/shard_map/mix/pallas_call | solution.py:456
  65.3 3.4 %all-to-all-done.1 = f32[16,1,128]{2,1,0:T(1,128)S(1)} async-done(((f32[16,1,128]{2,1,0:T(1,128)}), f32[16,1,128]{2,1,0:T(1,128)S(1)}, u32[]{:S(2)}, u32[]{:S(2)}) %all-to-all-start.1) | async-done | bytes 8224 | tf_op jit(solution)/shard_map/all_to_all | solution.py:449
  68.6 1.0 wave.1
  69.6 29.9 %all_to_all.26.y_ref = bf16[48,40,128]{2,1,0:T(8,128)(2,1)S(1)} all-to-all(bf16[48,40,128]{2,1,0:T(8,128)(2,1)S(1)} %get-tuple-element.25), channel_id=1, replica_groups=mesh['lat'=48,'fld'=16] {'lat'}, dimensions={0} | all-to-all | bytes 983040 | tf_op jit(solution)/shard_map/all_to_all | solution.py:499
  99.5 1.4 %scatter.1 = bf16[16,40,128]{2,1,0:T(8,128)(2,1)} custom-call(bf16[48,40,128]{2,1,0:T(8,128)(2,1)S(1)} %all_to_all.26.y_ref), custom_call_target="tpu_custom_call" | custom-call | flops 100000000 | bytes 2000000 | tf_op jit(solution)/shard_map/scatter/pallas_call | solution.py:502
  100.9 4.8 %all-to-all-start.3 = ((bf16[16,40,128]{2,1,0:T(8,128)(2,1)}), bf16[16,40,128]{2,1,0:T(8,128)(2,1)S(1)}, u32[]{:S(2)}, u32[]{:S(2)}) async-start(bf16[16,40,128]{2,1,0:T(8,128)(2,1)} %scatter.1), calls=%async_computation.3 | async-start | bytes 327680 | tf_op jit(solution)/shard_map/all_to_all | solution.py:512
  106.4 1.4 %wide.1.wide_ref = bf16[1536,640]{1,0:T(8,128)(2,1)S(1)} custom-call(s32[1,768]{1,0:T(1,128)S(1)} %broadcast_in_dim.19.wave_ref), custom_call_target="tpu_custom_call" | custom-call | flops 6000000 | bytes 3000000 | tf_op jit(solution)/shard_map/wide/pallas_call | solution.py:515
  107.8 1.9 %synthesis.1.d_ref = bf16[2,72,2560]{2,1,0:T(8,128)(2,1)S(1)} custom-call(bf16[48,40,128]{2,1,0:T(8,128)(2,1)S(1)} %all_to_all.26.y_ref, s32[1,768]{1,0:T(1,128)S(1)} %broadcast_in_dim.19.wave_ref, bf16[1536,640]{1,0:T(8,128)(2,1)S(1)} %wide.1.wide_ref), custom_call_target="tpu_custom_call" | custom-call | flops 1200000000 | bytes 6000000 | tf_op jit(solution)/shard_map/synthesis/pallas_call | solution.py:524
  109.7 5.1 %all-to-all-done.3.part_ref = bf16[16,40,128]{2,1,0:T(8,128)(2,1)S(1)} async-done(((bf16[16,40,128]{2,1,0:T(8,128)(2,1)}), bf16[16,40,128]{2,1,0:T(8,128)(2,1)S(1)}, u32[]{:S(2)}, u32[]{:S(2)}) %all-to-all-start.3) | async-done | bytes 163872 | tf_op jit(solution)/shard_map/all_to_all | solution.py:512
  114.8 1.1 final.1
  (10 shorter events, 0.1 us)
Async XLA Ops:
  0.6 59.3 %collective-permute-start.1 = (bf16[1044,128]{1,0:T(8,128)(2,1)}, bf16[1044,128]{1,0:T(8,128)(2,1)S(1)}, u32[]{:S(2)}, u32[]{:S(2)}) collective-permute-start(bf16[1044,128]{1,0:T(8,128)(2,1)} %state_ref.1), channel_id=1, source_target_pairs={{0,1},{1,2},{2,3},{3,4},{4,5},{5,6},{6,7},{7,8},{8,9},{9,10},{10,1... | collective-permute-start | bytes 801800 | tf_op jit(solution)/shard_map/ppermute | solution.py:434
  4.7 55.2 %collective-permute-start.2 = (bf16[1044,128]{1,0:T(8,128)(2,1)}, bf16[1044,128]{1,0:T(8,128)(2,1)S(1)}, u32[]{:S(2)}, u32[]{:S(2)}) collective-permute-start(bf16[1044,128]{1,0:T(8,128)(2,1)} %state_ref.1), channel_id=1, source_target_pairs={{1,0},{2,1},{3,2},{4,3},{5,4},{6,5},{7,6},{8,7},{9,8},{10,9},{11,1... | collective-permute-start | bytes 801800 | tf_op jit(solution)/shard_map/ppermute | solution.py:435
  11.5 20.7 %copy-start.6 = (s32[768]{0:T(1024)S(1)}, s32[768]{0:T(1024)}, u32[]{:S(2)}) copy-start(s32[768]{0:T(1024)} %wave_ref.1) | copy-start | bytes 9220
  11.5 21.0 %copy-start.8 = (f32[1044]{0:T(1024)S(1)}, f32[1044]{0:T(1024)}, u32[]{:S(2)}) copy-start(f32[1044]{0:T(1024)} %param.18) | copy-start | bytes 12532
  11.5 21.0 %copy-start.7 = (s32[2048]{0:T(1024)S(1)}, s32[2048]{0:T(1024)}, u32[]{:S(2)}) copy-start(s32[2048]{0:T(1024)} %param.21) | copy-start | bytes 24580
  11.5 21.2 %copy-start.5 = (bf16[1044,16]{0,1:T(8,128)(2,1)S(1)}, bf16[1044,16]{0,1:T(8,128)(2,1)}, u32[]{:S(2)}) copy-start(bf16[1044,16]{0,1:T(8,128)(2,1)} %param.16) | copy-start | bytes 100228
  11.6 21.4 %copy-start.9 = (f32[1044]{0:T(1024)S(1)}, f32[1044]{0:T(1024)}, u32[]{:S(2)}) copy-start(f32[1044]{0:T(1024)} %param.19) | copy-start | bytes 12532
  17.0 25.9 %all-to-all-start = ((bf16[24,24,128]{2,1,0:T(8,128)(2,1)}), bf16[24,24,128]{2,1,0:T(8,128)(2,1)S(1)}, u32[]{:S(2)}, u32[]{:S(2)}) async-start(bf16[24,24,128]{2,1,0:T(8,128)(2,1)} %get-tuple-element.16), calls=%async_computation | async-start | bytes 294912 | tf_op jit(solution)/shard_map/all_to_all | solution.py:416
  42.9 6.0 %collective-permute-start = (bf16[24,24,128]{2,1,0:T(8,128)(2,1)S(1)}, bf16[24,24,128]{2,1,0:T(8,128)(2,1)S(1)}, u32[]{:S(2)}, u32[]{:S(2)}) collective-permute-start(bf16[24,24,128]{2,1,0:T(8,128)(2,1)S(1)} %all-to-all-done.own_ref), channel_id=1, source_target_pairs={{0,16},{16,0},{32,48},{48,32},{64,80},{80,64},{96,112},{112,96},{1... | collective-permute-start | bytes 442376 | tf_op jit(solution)/shard_map/ppermute | solution.py:419
  48.8 11.1 %copy-start.1 = (bf16[1044,128]{1,0:T(8,128)(2,1)S(1)}, bf16[1044,128]{1,0:T(8,128)(2,1)}, u32[]{:S(2)}) copy-start(bf16[1044,128]{1,0:T(8,128)(2,1)} %state_ref.1) | copy-start | bytes 801796
  48.8 11.1 %copy-start.2 = (s32[512]{0:T(512)S(1)}, s32[512]{0:T(512)}, u32[]{:S(2)}) copy-start(s32[512]{0:T(512)} %param.22) | copy-start | bytes 6148
  48.8 11.1 %copy-start.3 = (s32[512]{0:T(512)S(1)}, s32[512]{0:T(512)}, u32[]{:S(2)}) copy-start(s32[512]{0:T(512)} %param.23) | copy-start | bytes 6148
  53.5 9.7 %copy-start = (bf16[1536,144]{1,0:T(8,128)(2,1)S(1)}, bf16[1536,144]{1,0:T(8,128)(2,1)}, u32[]{:S(2)}) copy-start(bf16[1536,144]{1,0:T(8,128)(2,1)} %get-tuple-element.22.f_ref) | copy-start | bytes 1327108
  53.5 9.7 %copy-start.4 = (f32[72]{0:T(128)S(1)}, f32[72]{0:T(128)}, u32[]{:S(2)}) copy-start(f32[72]{0:T(128)} %mix_ref.1) | copy-start | bytes 868
  53.5 15.1 %all-to-all-start.1 = ((f32[16,1,128]{2,1,0:T(1,128)}), f32[16,1,128]{2,1,0:T(1,128)S(1)}, u32[]{:S(2)}, u32[]{:S(2)}) async-start(f32[16,1,128]{2,1,0:T(1,128)} %bitcast.4), calls=%async_computation.1 | async-start | bytes 16384 | tf_op jit(solution)/shard_map/all_to_all | solution.py:449
  100.9 13.9 %all-to-all-start.3 = ((bf16[16,40,128]{2,1,0:T(8,128)(2,1)}), bf16[16,40,128]{2,1,0:T(8,128)(2,1)S(1)}, u32[]{:S(2)}, u32[]{:S(2)}) async-start(bf16[16,40,128]{2,1,0:T(8,128)(2,1)} %scatter.1), calls=%async_computation.3 | async-start | bytes 327680 | tf_op jit(solution)/shard_map/all_to_all | solution.py:512
